TPU v7x, 128 devices: a whole 4x4x4 slice. The times are simulated.
128 devices in a mesh: batch: 8 (over y, core), seq: 16 (over x, z).
Axes of the slice: x: 4, y: 4, z: 4, core: 2. Of those that a mesh axis runs over, the one named last changes fastest.
Arguments:
- feats: bfloat16 [16, 1024, 512], P('batch', 'seq'), may hold values from -6 to 6
- lengths: int32 [16], P('batch'), may hold values from 256 to 1024, as said below
- skip_flag: int32 [8], P('batch'), may hold values from 0 to 1, as said below
- cotangent: bfloat16 [16, 1024, 768], P('batch', 'seq'), may hold values from -6 to 6
- input_gain: bfloat16 [512], replicated, may hold values from 0.5 to 1.5
- input_shift: bfloat16 [512], replicated, may hold values from -3 to 3
- proj_weight: bfloat16 [512, 768], replicated, may hold values from -0.25 to 0.25
- proj_bias: bfloat16 [768], replicated, may hold values from -3 to 3
- conv_weight: bfloat16 [768, 48, 128], replicated, may hold values from -0.078125 to 0.078125
- conv_bias: bfloat16 [768], replicated, may hold values from -3 to 3
- encoder_gain: bfloat16 [768], replicated, may hold values from 0.5 to 1.5
- encoder_shift: bfloat16 [768], replicated, may hold values from -3 to 3
- qkv_weight: bfloat16 [768, 2304], replicated, may hold values from -0.21875 to 0.21875
- query_bias: bfloat16 [768], replicated, may hold values from -3 to 3
- value_bias: bfloat16 [768], replicated, may hold values from -3 to 3
- output_weight: bfloat16 [768, 768], replicated, may hold values from -3.5 to 3.5
- output_bias: bfloat16 [768], replicated, may hold values from -3 to 3
- middle_gain: bfloat16 [768], replicated, may hold values from 0.5 to 1.5
- middle_shift: bfloat16 [768], replicated, may hold values from -3 to 3
- inner_weight: bfloat16 [768, 3072], replicated, may hold values from -0.21875 to 0.21875
- inner_bias: bfloat16 [3072], replicated, may hold values from -3 to 3
- outer_weight: bfloat16 [3072, 768], replicated, may hold values from -0.109375 to 0.109375
- outer_bias: bfloat16 [768], replicated, may hold values from -3 to 3
- final_gain: bfloat16 [768], replicated, may hold values from 0.5 to 1.5
- final_shift: bfloat16 [768], replicated, may hold values from -3 to 3
Outputs:
- activations: bfloat16 [16, 1024, 768], P('batch', 'seq')
- grad_feats: float32 [16, 1024, 512], P('batch', 'seq')
- grad_input_gain: float32 [512], P(('batch', 'seq'))
- grad_input_shift: float32 [512], P(('batch', 'seq'))
- grad_proj_weight: float32 [512, 768], P(('batch', 'seq'))
- grad_proj_bias: float32 [768], P(('batch', 'seq'))
- grad_conv_weight: float32 [768, 48, 128], P(('batch', 'seq'))
- grad_conv_bias: float32 [768], P(('batch', 'seq'))
- grad_encoder_gain: float32 [768], P(('batch', 'seq'))
- grad_encoder_shift: float32 [768], P(('batch', 'seq'))
- grad_qkv_weight: float32 [768, 2304], P(('batch', 'seq'))
- grad_query_bias: float32 [768], P(('batch', 'seq'))
- grad_value_bias: float32 [768], P(('batch', 'seq'))
- grad_output_weight: float32 [768, 768], P(('batch', 'seq'))
- grad_output_bias: float32 [768], P(('batch', 'seq'))
- grad_middle_gain: float32 [768], P(('batch', 'seq'))
- grad_middle_shift: float32 [768], P(('batch', 'seq'))
- grad_inner_weight: float32 [768, 3072], P(('batch', 'seq'))
- grad_inner_bias: float32 [3072], P(('batch', 'seq'))
- grad_outer_weight: float32 [3072, 768], P(('batch', 'seq'))
- grad_outer_bias: float32 [768], P(('batch', 'seq'))
- grad_final_gain: float32 [768], P(('batch', 'seq'))
- grad_final_shift: float32 [768], P(('batch', 'seq'))
Inputs may be any that keep to these rules, and one draw needn't show every extreme that they name: `lengths`: in each bucket of 2 utterances one, chosen by the seed, has all 1024 frames. `skip_flag`: at least one bucket keeps the feed-forward branch and at least one drops it.
All inputs are finite; a program needn't handle non-finite values.
Results may differ from a plain program's by a relative error of at most 0.0208.
Values may be sent and summed in bfloat16 or wider, within the bound.
No kernel may reach another device: no remote copies, remote signals or barrier semaphores. Data moves between devices by JAX's collectives and lax.ppermute only.
A program may use at most 704 MiB of HBM per device.

v0:
```python
import functools

import jax
import jax.numpy as jnp
from jax import lax
from jax.experimental import pallas as pl
from jax.experimental.pallas import tpu as pltpu
from jax.sharding import PartitionSpec as P

f32 = jnp.float32
bf16 = jnp.bfloat16
i32 = jnp.int32

norm_eps = 1e-05
head_scale = 0.125
neg_fill = -1e30

D = 768
C_IN = 512
FF = 3072
GROUPS = 16
GW = 48
KW = 128
SUPER = 8
SW = SUPER * GW
TAP_BLOCKS = 17
BAND = TAP_BLOCKS * SW
ROWS = 128
SEQ = 16
PAIRS = 6
MIB = 1024 * 1024
TRANSPOSE_SCRATCH = pltpu.VMEM((D, 128), f32)

def nn(a, b):
    return lax.dot_general(a, b, (((1,), (0,)), ((), ())), preferred_element_type=f32)


def nt(a, b):
    return lax.dot_general(a, b, (((1,), (1,)), ((), ())), preferred_element_type=f32)


def tn(a, b):
    return lax.dot_general(a, b, (((0,), (0,)), ((), ())), preferred_element_type=f32)


def iota(shape, dim):
    return lax.broadcasted_iota(i32, shape, dim)


def int_div(x, c):
    return ((x.astype(f32) + 0.5) * (1.0 / c)).astype(i32)


def stats(x):
    c = x - jnp.mean(x, axis=-1, keepdims=True)
    r = lax.rsqrt(jnp.mean(c * c, axis=-1, keepdims=True) + norm_eps)
    return c * r, r


def norm_back(xhat, r, gain, g):
    e = g * gain
    dx = r * (e - jnp.mean(e, axis=-1, keepdims=True) - xhat * jnp.mean(e * xhat, axis=-1, keepdims=True))
    return dx, jnp.sum(g * xhat, axis=0, keepdims=True), jnp.sum(g, axis=0, keepdims=True)


def normal(x):
    bell = jnp.exp(-0.5 * x * x)
    t = 1.0 / (1.0 + (0.3275911 * 0.7071067811865476) * jnp.abs(x))
    poly = t * (0.127414796 + t * (-0.142248368 + t * (0.7107068705 + t * (-0.7265760135 + t * 0.5307027145))))
    tail = poly * bell
    return jnp.where(x < 0, tail, 1.0 - tail), 0.3989422804014327 * bell


def gelu(x):
    return x * normal(x)[0]


def gelu_slope(x):
    c, density = normal(x)
    return c + x * density


def col_sum(x):
    return jnp.sum(x.astype(f32), axis=0, keepdims=True)


def vec(lazy):
    ref = lazy()
    return ref[...].astype(f32).reshape(1, ref.shape[0])


def swap_blocks(xs):
    ys = [pltpu.roll(x, f * GW, 1) if f else x for f, x in enumerate(xs)]
    lane = iota((16, 128), 1)
    outs = []
    for g in range(SUPER):
        tiles = []
        for v in range(SW // 128):
            lo, hi = (128 * v) // GW, (128 * v + 127) // GW
            tile = ys[(lo - g) % SUPER][:, v * 128 : (v + 1) * 128]
            for q in range(lo + 1, hi + 1):
                tile = jnp.where(lane >= q * GW - 128 * v, ys[(q - g) % SUPER][:, v * 128 : (v + 1) * 128], tile)
            tiles.append(tile)
        w = jnp.concatenate(tiles, axis=1)
        outs.append(pltpu.roll(w, SW - g * GW, 1) if g else w)
    return outs


LANE_TILES = D // 128


def rows_to_groups(x, scratch):
    for v in range(LANE_TILES):
        scratch[v * ROWS : (v + 1) * ROWS, :] = x[:, v * 128 : (v + 1) * 128]
    outs = []
    for half in range(2):
        tiles = range(half * 3, half * 3 + 3)
        outs += swap_blocks(
            [
                jnp.concatenate([scratch[pl.ds(v * ROWS + f, 16, stride=SUPER), :] for v in tiles], axis=1)
                for f in range(SUPER)
            ]
        )
    return outs


def groups_to_rows(in_ref, scratch):
    for half in range(2):
        xs = [in_ref[half * 8 + g].astype(f32) for g in range(SUPER)]
        for f, x in enumerate(swap_blocks(xs)):
            for v in range(3):
                row = (half * 3 + v) * ROWS + f
                scratch[pl.ds(row, 16, stride=SUPER), :] = x[:, v * 128 : (v + 1) * 128]
    return jnp.concatenate([scratch[v * ROWS : (v + 1) * ROWS, :] for v in range(LANE_TILES)], axis=1)


class Hbm:
    def __init__(self, array):
        self.array = array


class Raw(Hbm):
    pass


class Smem(Hbm):
    pass


class Spill:
    def __init__(self, dims, dtype, parts=1):
        self.struct, self.parts = jax.ShapeDtypeStruct(dims, dtype), parts


class Copy:
    parts = 1

    def __init__(self, dims, dtype, operand):
        self.struct, self.operand = jax.ShapeDtypeStruct(dims, dtype), operand


class Flusher:
    def __init__(self, ref, target, sems, base, copies):
        self.ref, self.target, self.sems, self.next, self.copies = ref, target, sems, base, copies

    def put(self, value):
        self.ref[...] = value
        self.flush()

    def flush(self, *index):
        src, dst = (self.ref.at[index], self.target.at[index]) if index else (self.ref, self.target)
        copy = pltpu.make_async_copy(src, dst, self.sems.at[self.next])
        copy.start()
        self.next += 1
        self.copies.append(copy)


class Lazy:
    def __init__(self, copy, ref):
        self.copy, self.ref, self.waited = copy, ref, False

    def __call__(self):
        if not self.waited:
            self.copy.wait()
            self.waited = True
        return self.ref


def call(body, outs, *args, scratch=(), flops=0, name=None, mib=16):
    fetched = [k for k, a in enumerate(args) if type(a) in (Hbm, Smem)]
    spilled = [k for k, o in enumerate(outs) if isinstance(o, Spill)]
    copied = [k for k, o in enumerate(outs) if isinstance(o, Copy)]
    arrays = [
        pltpu.with_memory_space_constraint(a.array, pltpu.HBM) if isinstance(a, Hbm) and not isinstance(a, Smem) else getattr(a,'array',a) for a in args
    ]
    structs = [o.struct if isinstance(o, (Spill, Copy)) else o for o in outs]
    near = {Hbm: pltpu.VMEM, Smem: pltpu.SMEM}
    own = [near[type(args[k])](arrays[k].shape, arrays[k].dtype) for k in fetched]
    own += [pltpu.VMEM(structs[k].shape, structs[k].dtype) for k in spilled]
    sem_count = len(fetched) + sum(outs[k].parts for k in spilled) + len(copied)
    if sem_count:
        own.append(pltpu.SemaphoreType.DMA((sem_count,)))

    def wrapped(*refs):
        n_in, n_out = len(args), len(outs)
        ins, out_refs, rest = list(refs[:n_in]), list(refs[n_in : n_in + n_out]), list(refs[n_in + n_out :])
        extra, rest = rest[: len(own)], rest[len(own) :]
        lazies, flushed = [], []
        for slot, k in enumerate(fetched):
            copy = pltpu.make_async_copy(ins[k], extra[slot], extra[-1].at[slot])
            copy.start()
            ins[k] = Lazy(copy, extra[slot])
            lazies.append(ins[k])
        base = len(fetched)
        for slot, k in enumerate(spilled):
            out_refs[k] = Flusher(extra[len(fetched) + slot], out_refs[k], extra[-1], base, flushed)
            base += outs[k].parts
        for k in copied:
            out_refs[k] = Flusher(refs[outs[k].operand], out_refs[k], extra[-1], base, flushed)
            base += 1
        body(*ins, *out_refs, *rest)
        for lazy in lazies:
            lazy()
        for copy in flushed:
            copy.wait()

    bytes_accessed = sum(a.size * a.dtype.itemsize for a in arrays) + sum(o.size * o.dtype.itemsize for o in structs)
    return pl.pallas_call(
        wrapped,
        out_shape=[pltpu.HBM(o.struct.shape, o.struct.dtype) if isinstance(o, (Spill, Copy)) else o for o in outs],
        in_specs=[pl.BlockSpec(memory_space=pltpu.HBM if isinstance(a, Hbm) else pltpu.VMEM) for a in args],
        out_specs=[pl.BlockSpec(memory_space=pltpu.HBM if isinstance(o, (Spill, Copy)) else pltpu.VMEM) for o in outs],
        scratch_shapes=own + list(scratch),
        compiler_params=pltpu.CompilerParams(vmem_limit_bytes=mib * MIB),
        cost_estimate=pl.CostEstimate(flops=flops, bytes_accessed=bytes_accessed, transcendentals=0),
        name=name,
    )(*arrays)


def fetch(sems, *pairs):
    copies = [pltpu.make_async_copy(src, dst, sems.at[k]) for k, (src, dst) in enumerate(pairs)]
    for copy in copies:
        copy.start()
    return copies


def shape(dims, dtype):
    return jax.ShapeDtypeStruct(dims, dtype)


def live_rows(lengths):
    row = iota((ROWS, 1), 0)
    frame = (row & 63) + lax.axis_index("seq") * 64
    ref = lengths()
    length = jnp.where(row < 64, ref[0], ref[1])
    return (frame < length).astype(f32)


def head_utterance():
    return (lax.axis_index("seq") >= PAIRS).astype(i32)


def core_index():
    return lax.axis_index("batch") & 1


def project_kernel(lengths, feats, gain, shift, weight, bias, masked_out, send_out, scratch):
    xhat, _ = stats(feats()[...].astype(f32))
    normed = (xhat * vec(gain) + vec(shift)).astype(bf16)
    masked = (nn(normed, weight()[...]) + vec(bias)) * live_rows(lengths)
    masked_out.put(masked)
    for g, x in enumerate(rows_to_groups(masked, scratch)):
        send_out[g] = x.astype(bf16)


def band_rows(taps):
    flat = jnp.concatenate([taps[...].astype(f32), jnp.zeros((GW, SW), f32)], axis=1)
    return [(pltpu.roll(flat, f * GW, 1) if f else flat).astype(bf16) for f in range(SUPER)]


def padded(pieces, scratch):
    for u in range(2):
        scratch[u, 0:8, :] = jnp.zeros((8, SW), f32)
        scratch[u, 136:144, :] = jnp.zeros((8, SW), f32)
        for p, x in enumerate(pieces):
            scratch[u, 8 + p * 8 : 16 + p * 8, :] = x[u * 8 : u * 8 + 8]


def windows(scratch, starts):
    parts = [
        jnp.concatenate([scratch[u, start : start + 128, :] for u in range(2)], axis=0).astype(bf16) for start in starts
    ]
    return jnp.concatenate(parts, axis=1)


def by_seq(x, p):
    return jnp.concatenate([x[u * 128 + p * 8 : u * 128 + p * 8 + 8] for u in range(2)], axis=0)


def conv_kernel(x, taps, out, x_out, w, scratch):
    x_out.flush()
    for f, rows in enumerate(band_rows(taps())):
        w[f * GW : (f + 1) * GW, :] = rows
    padded([x[p].astype(f32) for p in range(SEQ)], scratch)
    res = nt(windows(scratch, range(TAP_BLOCKS)), w[...])
    for p in range(SEQ):
        out[p] = by_seq(res, p).astype(bf16)


CHUNK = 56


def conv_back_kernel(lengths, got_in, taps, out, w, scratch):
    for f, rows in enumerate(band_rows(taps())):
        for i in range(TAP_BLOCKS):
            w[i * SW + f * GW : i * SW + (f + 1) * GW, :] = rows[:, i * SW : (i + 1) * SW]
    got = got_in()
    padded([got[p, :16, :].astype(f32) for p in range(SEQ)], scratch)
    res = nn(windows(scratch, range(16, -1, -1)), w[...])
    row, f = iota((16, SW), 0), int_div(iota((1, SW), 1), GW)
    ref = lengths()
    length = jnp.where(row < 8, ref[0], ref[1])
    for p in range(SEQ):
        total = by_seq(res, p) + got[p, 16:, :].astype(f32)
        live = p * 64 + (row & 7) * SUPER + f < length
        out[p] = jnp.where(live, total, 0.0).astype(bf16)


def conv_weight_kernel(got_in, other_in, x_in, x_other, *rest):
    tap_outs, (wide, acc, spread, chunks, scratch) = rest[:4], rest[4:]
    core = core_index()
    src, dst = iota((SW, 192), 0), iota((1, 192), 1)
    f = int_div(dst, 24)
    y = int_div(dst - 24 * f, 6)
    own_taps = (src == f * GW + (2 * y + core) * 6 + (dst - 24 * f - 6 * y)).astype(f32).astype(bf16)
    grads, parts = [], []
    for k, (got, x) in enumerate(((got_in(), x_in()), (other_in(), x_other()))):
        grad = jnp.concatenate([got[p, :16, :] for p in range(SEQ)], axis=0)
        grad = nn(grad, own_taps)
        grads.append(jnp.concatenate([grad[p * 16 + u * 8 : p * 16 + u * 8 + 8] for u in range(2) for p in range(SEQ)], axis=0))
        padded([x[p].astype(f32) for p in range(SEQ)], scratch.at[k])
        parts.append(windows(scratch.at[k], range(TAP_BLOCKS)))
    wide[...] = nn(jnp.concatenate(grads, axis=0).astype(bf16).T, jnp.concatenate(parts, axis=0))
    acc[...] = wide[7 * 24 :, :]
    for f in range(6, -1, -1):
        acc[...] = pltpu.roll(acc[...], BAND - GW, 1) + wide[f * 24 : f * 24 + 24, :]
    for v in range(LANE_TILES):
        lanes = slice(v * 128, (v + 1) * 128)
        for i in range(8):
            spread[pl.ds(i, 24, stride=8), :] = acc[:, i * D + v * 128 : i * D + (v + 1) * 128]
        for y in range(4):
            chunks[y, :, lanes] = spread[y * GW : (y + 1) * GW, :].astype(bf16)
    own_y = lax.axis_index("batch") >> 1
    for k, tap_out in enumerate(tap_outs):
        tap_out.put(chunks[(own_y + k) & 3])


def conv_sum_kernel(*refs):
    total = refs[0]()[...].astype(f32)
    for ref in refs[1:-1]:
        total += ref()[...].astype(f32)
    refs[-1][...] = total


def dense_sum_kernel(total_in, inner_out, outer_out, output_out):
    total = total_in()[...].astype(f32)
    for q in range(4):
        inner_out[:, q * D : (q + 1) * D] = total[q * 6 : q * 6 + 6]
    output_out[...] = total[24:30]
    outer_out[...] = total[32:]


def qkv_kernel(
    conv, masked, conv_bias, gain, shift, weight, query_bias, value_bias, feats,
    pre_out, hidden_out, send_out, rows_out, scratch,
):
    pre = groups_to_rows(conv, scratch) + vec(conv_bias)
    pre_out.put(pre)
    xhat, _ = stats(masked()[...] + gelu(pre))
    hidden = xhat * vec(gain) + vec(shift)
    hidden_out.put(hidden)
    hidden_b = hidden.astype(bf16)
    rows_out.ref[:, :D] = hidden_b
    rows_out.ref[:, D:] = feats()[...]
    rows_out.flush()
    zero = jnp.zeros((1, D), f32)
    send = send_out.ref
    for slot, (block, bias) in enumerate(((1, zero), (2, vec(value_bias)), (0, vec(query_bias)))):
        part = (nn(hidden_b, weight()[:, block * D : (block + 1) * D]) + bias).astype(bf16)
        for u in range(2):
            for pair in range(PAIRS):
                send[u * PAIRS + pair, slot * 64 : (slot + 1) * 64, :] = part[
                    u * 64 : (u + 1) * 64, pair * 128 : (pair + 1) * 128
                ]
        part_rows = slice(slot * 64, (slot + 1) * 64)
        send[2 * PAIRS :, part_rows, :] = jnp.zeros((SEQ - 2 * PAIRS, 64, 128), bf16)
        send_out.flush(slice(None), part_rows)


Q_BLOCK = 512


def columns(*values):
    rows = max(v.shape[0] for v in values)
    lane = iota((rows, 128), 1)
    out = jnp.zeros((rows, 128), f32)
    for k, v in enumerate(values):
        out = jnp.where(lane == k, v, out)
    return out.astype(bf16)


def three_terms(x):
    high = x.astype(bf16).astype(f32)
    mid = (x - high).astype(bf16).astype(f32)
    return high, mid, x - high - mid


def key_bias(lengths):
    ref = lengths()
    length = jnp.where(head_utterance() == 0, ref[0], ref[1])
    return jnp.where(iota((1024, 1), 0) < length, 0.0, neg_fill)


def attend_kernel(lengths, qkv, out, log_spill, out_spill, copy_spill):
    log_out, full_out = log_spill.ref, out_spill.ref
    copy_spill.flush()
    keys = jnp.concatenate([qkv[:, 0:64, :].reshape(1024, 128), columns(key_bias(lengths))], axis=1)
    values = jnp.concatenate([qkv[:, 64:128, :].reshape(1024, 128), columns(jnp.ones((1024, 1), f32))], axis=1)
    left = iota((1024, 128), 1) < 64
    query = qkv[:, 128:192, :].reshape(1024, 128) * head_scale
    parts, logs = [], []
    for head in range(2):
        own = left if head == 0 else ~left
        q_h = jnp.concatenate([jnp.where(own, query, jnp.zeros_like(query)), columns(jnp.ones((1024, 1), f32))], axis=1)
        scores = nt(q_h, keys)
        top = jnp.max(scores, axis=-1, keepdims=True)
        e = jnp.exp(scores - top).astype(bf16)
        sums = nn(e, values)
        total = sums[:, 128:129]
        parts.append(sums[:, :128] * (1.0 / total))
        logs.append(top + jnp.log(total))
    both = jnp.where(left, parts[0], parts[1])
    out[...] = both.astype(bf16)
    full_out[...] = both
    log_out[...] = jnp.where(left, logs[0], logs[1])
    log_spill.flush()
    out_spill.flush()


def attend_back_kernel(lengths, qkv_in, grad, logs_in, full_in, spill, dk, dv, dq):
    qkv, logs, full, out = qkv_in(), logs_in(), full_in(), spill.ref
    one = jnp.ones((1024, 1), f32)
    keys_only = qkv[:, 0:64, :].reshape(1024, 128)
    keys = jnp.concatenate([keys_only, columns(key_bias(lengths), one, one, one)], axis=1)
    values = jnp.concatenate([qkv[:, 64:128, :].reshape(1024, 128), columns(one, one, one)], axis=1)
    keys_t = keys_only.T
    left = iota((Q_BLOCK, 128), 1) < 64
    top_rows = iota((128, Q_BLOCK), 0) < 64
    per = Q_BLOCK // 64
    dk[...] = jnp.zeros_like(dk)
    dv[...] = jnp.zeros_like(dv)
    dq[...] = jnp.zeros_like(dq)

    def step(n, carry):
        query = qkv[pl.ds(n * per, per), 128:192, :].reshape(Q_BLOCK, 128) * head_scale
        rows = pl.ds(pl.multiple_of(n * Q_BLOCK, Q_BLOCK), Q_BLOCK)
        go = grad[rows, :]
        weighted = go.astype(f32) * full[rows, :]
        def one_head(head, carry):
            own = (left & (head == 0)) | (~left & (head == 1))
            q_h = jnp.where(own, query, jnp.zeros_like(query))
            g_h = jnp.where(own, go, jnp.zeros_like(go))
            log = jnp.where(head == 0, logs[rows, 0:1], logs[rows, 64:65])
            delta = jnp.sum(jnp.where(own, weighted, 0.0), axis=-1, keepdims=True)
            q_more = jnp.concatenate([q_h, columns(jnp.ones((Q_BLOCK, 1), f32), *three_terms(-log))], axis=1)
            g_more = jnp.concatenate([g_h, columns(*three_terms(-delta))], axis=1)
            probs = jnp.exp(nt(keys, q_more))
            grad_scores = (probs * nt(values, g_more)).astype(bf16)
            head_rows = (top_rows & (head == 0)) | (~top_rows & (head == 1))
            dq[...] = jnp.where(head_rows, nn(keys_t, grad_scores), dq[...])
            dk[...] += nn(grad_scores, q_h)
            dv[...] += nn(probs.astype(bf16), g_h)
            return carry

        lax.fori_loop(0, 2, one_head, 0)
        grad_query = (dq[...] * head_scale).T.astype(bf16)
        out[pl.ds(n * per, per), 0:64, :] = grad_query.reshape(per, 64, 128)
        return carry

    lax.fori_loop(0, 1024 // Q_BLOCK, step, 0)
    out[:, 64:128, :] = dk[...].astype(bf16).reshape(SEQ, 64, 128)
    out[:, 128:192, :] = dv[...].astype(bf16).reshape(SEQ, 64, 128)
    spill.flush()


def frames_kernel(rows_in, gain, shift, normed_out, high_out, low_out, feats, sem):
    copy = pltpu.make_async_copy(rows_in.at[:, :, :, D : D + C_IN], feats, sem.at[0])
    copy.start()
    gain_row, shift_row = vec(gain), vec(shift)
    copy.wait()

    def step(p, carry):
        rows = pl.ds(pl.multiple_of(p * 128, 128), 128)
        xhat, _ = stats(feats[p].reshape(128, C_IN).astype(f32))
        normed_out.ref[rows, :] = (xhat * gain_row + shift_row).astype(bf16)
        high = xhat.astype(bf16)
        high_out.ref[rows, :] = high
        low_out.ref[rows, :] = (xhat - high.astype(f32)).astype(bf16)
        return carry

    lax.fori_loop(0, SEQ, step, 0)
    for spill in (normed_out, high_out, low_out):
        spill.flush()


def head_grads_kernel(rows_in, grads_in, spill, hidden, sem):
    copy = pltpu.make_async_copy(rows_in.at[:, head_utterance(), :, 0:D], hidden, sem.at[0])
    copy.start()
    grads = grads_in()
    right = jnp.concatenate([grads[:, k * 64 : (k + 1) * 64, :].reshape(1024, 128) for k in range(3)], axis=1)
    copy.wait()
    res = tn(hidden[...].reshape(1024, D), right).astype(bf16)

    def step(k, carry):
        rows = pl.ds(pl.multiple_of(k * 256, 256), 256)
        dst, src = iota((256, 1), 0) + k * 256, iota((256, D), 1)
        row = jnp.where((dst & 7) < 6, (dst >> 3) * 6 + (dst & 7), -1)
        spill.ref[rows, :] = nn((src == row).astype(f32).astype(bf16), res).astype(bf16)
        return carry

    lax.fori_loop(0, 4, step, 0)
    spill.flush()


def owner_order(core):
    src, dst = iota((D, D), 0), iota((1, D), 1)
    second = dst >= 384
    rest = dst - jnp.where(second, 384, 0)
    which = jnp.where(second, 1 - core, core)
    s = int_div(rest, 24)
    y = int_div(rest - 24 * s, 6)
    j = rest - 24 * s - 6 * y
    return (src == (2 * y + which) * 96 + s * 6 + j).astype(f32).astype(bf16)


S_MID, S_GI, S_INNER, S_GO, S_ATT, S_GA, S_END = 0, 384, 3456, 4992, 5760, 6144, 6912
O_MID, O_INNER, O_ATT, O_END = 0, 384, 1920, 2304


def middle_kernel(
    skip, recv, hidden, cot, out_w_in, out_b, mid_g_in, mid_s_in, inner_w_in, inner_b_in, outer_w_in, outer_b,
    fin_g_in, fin_s_in,
    act_out, grad_att_out, gmi_out, send_out, own_out, small_out,
    act, slope, out_w, inner_w, outer_w, bias, total, sems,
):
    pairs = [(out_w_in, out_w)]
    for q in range(4):
        cols = slice(q * D, (q + 1) * D)
        pairs += [(inner_w_in.at[:, cols], inner_w.at[:, cols]), (outer_w_in.at[cols, :], outer_w.at[cols, :])]
    copies = fetch(sems, *pairs)
    core = core_index()
    keep = (1 - skip()[0]).astype(f32)
    mid_gain, fin_gain, inner_bias = vec(mid_g_in), vec(fin_g_in), vec(inner_b_in)
    att = jnp.concatenate(
        [jnp.concatenate([recv[u * PAIRS + p] for p in range(PAIRS)], axis=1) for u in range(2)], axis=0
    )
    copies[0].wait()
    middle_in = hidden()[...] + nn(att, out_w[...]) + vec(out_b)
    xm, rm = stats(middle_in)
    middle = xm * mid_gain + vec(mid_s_in)
    middle_b = middle.astype(bf16)
    order = owner_order(core)
    mid = nn(middle_b, order).astype(bf16)
    att_p = nn(att, order).astype(bf16)
    own, send = own_out, send_out

    own[:, O_MID : O_MID + 384] = mid[:, :384]
    own[:, O_ATT : O_ATT + 384] = att_p[:, :384]
    send[:, S_MID : S_MID + 384] = mid[:, 384:]
    send[:, S_ATT : S_ATT + 384] = att_p[:, 384:]
    bias[0:1, :] = inner_bias
    total[...] = jnp.zeros_like(total)

    def block(q):
        return pl.ds(pl.multiple_of(q * D, D), D)

    def forward(q, carry):
        cols = block(q)
        pltpu.make_async_copy(inner_w_in.at[:, cols], inner_w.at[:, cols], sems.at[1 + 2 * q]).wait()
        pre = nn(middle_b, inner_w[:, cols]) + bias[0:1, cols]
        c, density = normal(pre)
        inner_b = (pre * c).astype(bf16)
        act[:, cols] = inner_b
        slope[:, cols] = c + pre * density
        pltpu.make_async_copy(outer_w_in.at[cols, :], outer_w.at[cols, :], sems.at[2 + 2 * q]).wait()
        total[...] += nn(inner_b, outer_w[cols, :])
        return carry

    lax.fori_loop(0, 4, forward, 0)
    outer = total[...]
    first = core == 0
    for y in range(4):
        even = act[:, 2 * y * 384 : (2 * y + 1) * 384]
        odd = act[:, (2 * y + 1) * 384 : (2 * y + 2) * 384]
        own[:, O_INNER + y * 384 : O_INNER + (y + 1) * 384] = jnp.where(first, even, odd)
        send[:, S_INNER + y * 384 : S_INNER + (y + 1) * 384] = jnp.where(first, odd, even)
    final_in = middle + keep * (outer + vec(outer_b))
    xf, rf = stats(final_in)
    act_out.put((xf * fin_gain + vec(fin_s_in)).astype(bf16))
    gfi, fin_g, fin_s = norm_back(xf, rf, fin_gain, cot()[...].astype(f32))
    grad_outer = (keep * gfi).astype(bf16)
    send[:, S_GO : S_GO + D] = grad_outer
    total[...] = gfi

    def backward(q, carry):
        cols = block(q)
        grad_inner = (slope[:, cols] * nt(grad_outer, outer_w[cols, :])).astype(bf16)
        send[:, pl.ds(pl.multiple_of(S_GI + q * D, 128), D)] = grad_inner
        small_out.ref[pl.ds(3 + q, 1), :] = col_sum(grad_inner)
        total[...] += nt(grad_inner, inner_w[:, cols])
        return carry

    lax.fori_loop(0, 4, backward, 0)
    grad_middle = total[...]
    gmi, mid_g, mid_s = norm_back(xm, rm, mid_gain, grad_middle)
    gmi_out.put(gmi)
    grad_attn = gmi.astype(bf16)
    send[:, S_GA : S_GA + D] = grad_attn
    grad_att = nt(grad_attn, out_w[...]).astype(bf16)
    for u in range(2):
        for p in range(PAIRS):
            grad_att_out.ref[u * PAIRS + p] = grad_att[u * 64 : (u + 1) * 64, p * 128 : (p + 1) * 128]
    grad_att_out.ref[2 * PAIRS :] = jnp.zeros((SEQ - 2 * PAIRS, 64, 128), bf16)
    grad_att_out.flush()
    for row, value in ((0, fin_g), (1, fin_s), (2, col_sum(grad_outer)), (7, mid_g), (8, mid_s), (9, col_sum(grad_attn))):
        small_out.ref[row : row + 1, :] = value
    small_out.ref[10:16, :] = jnp.zeros((6, D), f32)
    small_out.flush()


def dense_grads_kernel(own, sent, got, spill):
    out = spill.ref

    def right(start):
        return jnp.concatenate([sent[:, start : start + D], got[:, start : start + D]], axis=0)

    def left(start, theirs, width):
        return jnp.concatenate([own[:, start : start + width], got[:, theirs : theirs + width]], axis=0)

    mid = left(O_MID, S_MID, 384)
    mid_t = mid.T
    sixes = [nn(mid_t, right(S_GI + q * D)).astype(bf16) for q in range(4)]
    sixes.append(nn(left(O_ATT, S_ATT, 384).T, right(S_GA)).astype(bf16))
    outer = nn(left(O_INNER, S_INNER, 1536).T, right(S_GO))
    dst, src = iota((512, 480), 0), iota((1, 480), 1)
    q = int_div(src, 96)
    n = int_div(src - 96 * q, 6)
    j = src - 96 * q - 6 * n
    order = (dst == n * 32 + q * 6 + j).astype(f32).astype(bf16)
    for quarter in range(4):
        rows = slice(quarter * 96, quarter * 96 + 96)
        block = nn(order, jnp.concatenate([x[rows] for x in sixes], axis=0))
        for k in range(4):
            s = quarter * 4 + k
            for y in range(0, 4, 2):
                pieces = []
                for m in (y, y + 1):
                    pieces.append(block[(k * 4 + m) * 32 : (k * 4 + m) * 32 + 32])
                    pieces.append(outer[m * 384 + s * 24 : m * 384 + s * 24 + 24])
                out[s, y * CHUNK : (y + 2) * CHUNK, :] = jnp.concatenate(pieces, axis=0).astype(bf16)
        spill.flush(slice(quarter * 4, quarter * 4 + 4))


def qkv_back_kernel(
    recv, gmi, pre_in, masked, gain_in, weight, send_out, small_out, scratch
):
    pre = pre_in()[...]
    gain = vec(gain_in)
    xhat, r = stats(masked()[...] + gelu(pre))
    grad_hidden = gmi()[...]
    sums = []
    for slot in range(3):
        part = jnp.concatenate(
            [
                jnp.concatenate([recv[u * PAIRS + p, slot * 64 : (slot + 1) * 64, :] for p in range(PAIRS)], axis=1)
                for u in range(2)
            ],
            axis=0,
        )
        sums.append(col_sum(part))
        grad_hidden += nt(part, weight()[:, slot * D : (slot + 1) * D])
    grad_summed, enc_g, enc_s = norm_back(xhat, r, gain, grad_hidden)
    grad_conv = (gelu_slope(pre) * grad_summed).astype(bf16).astype(f32)
    for k, x in enumerate((grad_conv, grad_summed)):
        for g, rows in enumerate(rows_to_groups(x, scratch)):
            send_out[g, k * 16 : k * 16 + 16, :] = rows.astype(bf16)
    for row, value in enumerate((enc_g, enc_s, sums[0], sums[2], jnp.sum(grad_conv, axis=0, keepdims=True))):
        small_out.ref[row : row + 1, :] = value
    small_out.ref[5:8, :] = jnp.zeros((3, D), f32)
    small_out.flush()


def feats_back_kernel(grad, feats, gain_in, weight, feats_out, scratch):
    grad_proj = groups_to_rows(grad, scratch).astype(bf16)
    xhat, r = stats(feats()[...].astype(f32))
    feats_out[...] = norm_back(xhat, r, vec(gain_in), nt(grad_proj, weight()[...]))[0]


def tail_kernel(
    grad_in, small_a, small_b, weight, high, low, normed, qkv_rows, tail_out, frames, spread, by_four
):
    group = lax.axis_index("seq")
    lane = iota((1, 128), 1)
    ref = grad_in()
    grad = jnp.concatenate([ref[p].astype(f32) for p in range(SEQ)], axis=0)
    for f in range(SUPER):
        moved = pltpu.roll(grad, SW - f * GW, 1) if f else grad
        frames[pl.ds(f, 256, stride=SUPER), :] = jnp.where(lane < GW, moved[:, :128], 0.0)
    grads = frames[...].astype(bf16)
    grads_t = grads.T
    pick = (iota((128, D), 1) == iota((128, D), 0) + group * GW) & (iota((128, 1), 0) < GW)
    own_weight = nt(pick.astype(f32).astype(bf16), weight()[...])
    sums = jnp.sum(grads_t.astype(f32), axis=1, keepdims=True)
    in_g = jnp.sum(own_weight * (nn(grads_t, high()[...]) + nn(grads_t, low()[...])), axis=0, keepdims=True)
    in_s = jnp.sum(own_weight * sums, axis=0, keepdims=True)
    by_four[...] = nn(grads_t, normed()[...]).T
    bias = jnp.sum(grads.astype(f32), axis=0, keepdims=True)
    place = pick.astype(f32).astype(bf16)
    bias_high = bias.astype(bf16)
    bias_low = (bias - bias_high.astype(f32)).astype(bf16)
    proj_b = nn(jnp.concatenate([bias_high] * 8, axis=0), place) + nn(jnp.concatenate([bias_low] * 8, axis=0), place)
    a = lambda k: small_a()[k : k + 1, :]
    b = lambda k: small_b()[k : k + 1, :]
    vectors = [proj_b[:1], b(4), b(0), b(1), b(2), b(3), a(9), a(7), a(8), a(2), a(0), a(1)]
    lane6 = iota((1, D), 1)
    slot6 = lane6 - 6 * int_div(lane6, 6)
    sub = iota((8, D), 0)
    main = jnp.concatenate([jnp.where(slot6 == sub, v, 0.0) for v in vectors] + [jnp.zeros((32, D), f32)], axis=0)
    sub24 = iota((24, D), 0)
    slot24 = lane6 - 24 * int_div(lane6, 24)
    inner = [
        jnp.concatenate(
            [jnp.zeros((96, D), f32), jnp.where(slot24 == sub24, a(3 + k), 0.0), jnp.zeros((8, D), f32)], axis=0
        )
        for k in range(4)
    ]
    lane4, sub4 = iota((8, C_IN), 1) & 3, iota((8, C_IN), 0)
    last = jnp.concatenate(
        [
            jnp.zeros((120, C_IN), f32),
            jnp.where(lane4 == sub4, in_g, 0.0) + jnp.where(lane4 == sub4 - 4, in_s, 0.0),
        ],
        axis=0,
    )
    own = iota((128, D), 0)
    pick6 = (int_div(lane6, 6) == own).astype(f32).astype(bf16)
    pick24 = [(int_div(lane6, 24) + 32 * k == own).astype(f32).astype(bf16) for k in range(4)]
    pick4 = ((iota((1, C_IN), 1) >> 2) == iota((128, C_IN), 0)).astype(f32).astype(bf16)
    spread[...] = jnp.zeros_like(spread)
    both = jnp.zeros((128, 256), f32)
    for p, m in [(pick6, main)] + list(zip(pick24, inner)) + [(pick4, last)]:
        high_m = m.astype(bf16)
        low_m = (m - high_m.astype(f32)).astype(bf16)
        both += nt(p, jnp.concatenate([high_m, low_m], axis=0))
    for k in range(2):
        spread[pl.ds(k * 1024 + 6, 128, stride=8), :] = both[:, k * 128 : (k + 1) * 128]
    for k in range(2):
        first, second = [by_four[pl.ds(2 * k + n, 128, stride=4), :] for n in range(2)]
        spread[pl.ds(2048 + 6 + k, 128, stride=8), :] = first + pltpu.roll(second, GW, 1)
    rows = qkv_rows()
    for k in range(3):
        lanes = slice(k * 128, (k + 1) * 128)
        tail_out[:, lanes] = (rows[:, lanes].astype(f32) + spread[k * 1024 : (k + 1) * 1024, :]).astype(bf16)


def tail_sum_kernel(got, qkv_out, proj_out, *vector_outs):
    small = jnp.zeros((1, 128), f32)
    proj = [jnp.zeros((1, D), f32)] * 4
    sums = []
    for d in range(SEQ):
        total = got[d].astype(f32)
        for b in range(1, 8):
            total += got[b * SEQ + d].astype(f32)
        sums.append(total)
        small += total[6:7, :128] + total[6:7, 128:256]
        for k in range(4):
            piece = total[6 + k // 2 : 7 + k // 2, 256:]
            wide = jnp.concatenate([piece, jnp.zeros((1, D - 128), f32)], axis=1)
            shift = (d * GW - (k % 2) * GW) % D
            lane = iota((1, D), 1)
            start = (k % 2) * GW
            wide = jnp.where((lane >= start) & (lane < start + GW), wide, 0.0)
            proj[k] += pltpu.roll(wide, shift, 1) if shift else wide
    for p in range(PAIRS):
        pair = sums[p] + sums[PAIRS + p]
        for k in range(3):
            start = k * D + p * 128
            qkv_out[:, start : start + 128] = pair[:6, k * 128 : (k + 1) * 128]
    for k in range(4):
        proj_out[k : k + 1, :] = proj[k]
    starts = [120, 124] + [8 * k for k in range(7)] + [56, 64, 96, 72, 80, 88]
    for start, out in zip(starts, vector_outs):
        out[...] = small[0, start : start + out.shape[0]]


def to_peers(x, axis, groups=None):
    return lax.all_to_all(x, axis, 0, 0, tiled=True, axis_index_groups=groups)


Y_GROUPS = [[0, 2, 4, 6], [1, 3, 5, 7]]


def local(
    feats, lengths, skip_flag, cotangent, input_gain, input_shift, proj_weight, proj_bias, conv_weight, conv_bias,
    encoder_gain, encoder_shift, qkv_weight, query_bias, value_bias, output_weight, output_bias, middle_gain,
    middle_shift, inner_weight, inner_bias, outer_weight, outer_bias, final_gain, final_shift,
):
    seq = lax.axis_index("seq")
    rows_in = feats.reshape(ROWS, C_IN)
    cot = cotangent.reshape(ROWS, D)

    masked, conv_send = call(
        project_kernel,
        [Spill((ROWS, D), f32), shape((GROUPS, 16, SW), bf16)],
        Smem(lengths), Hbm(rows_in), Hbm(input_gain), Hbm(input_shift), Hbm(proj_weight), Hbm(proj_bias),
        flops=2 * ROWS * C_IN * D, name="project", scratch=[TRANSPOSE_SCRATCH],
    )
    conv_x = to_peers(conv_send, "seq")
    own_taps = lax.dynamic_slice_in_dim(conv_weight, seq * GW, GW, axis=0)
    taps = own_taps.transpose(0, 2, 1).reshape(GW, KW * GW)
    shifted = pltpu.VMEM((2, 144, SW), f32)
    conv_flops = 2 * 256 * SW * BAND
    conv_y, conv_x = call(
        conv_kernel, [shape((SEQ, 16, SW), bf16), Copy((SEQ, 16, SW), bf16, 0)], conv_x, Hbm(taps),
        scratch=[pltpu.VMEM((SW, BAND), bf16), shifted],
        flops=conv_flops, name="conv", mib=24,
    )
    conv_back = to_peers(conv_y, "seq")
    conv_pre, hidden, qkv_send, rows_send = call(
        qkv_kernel,
        [
            Spill((ROWS, D), f32), Spill((ROWS, D), f32), Spill((SEQ, 192, 128), bf16, parts=3),
            Spill((ROWS, D + C_IN), bf16),
        ],
        conv_back, Hbm(masked), Hbm(conv_bias), Hbm(encoder_gain), Hbm(encoder_shift), Hbm(qkv_weight), Hbm(query_bias),
        Hbm(value_bias), Hbm(rows_in), flops=2 * ROWS * D * 3 * D, name="qkv", scratch=[TRANSPOSE_SCRATCH],
    )
    qkv = to_peers(qkv_send, "seq")
    rows_all = lax.all_gather(rows_send, "seq", axis=0, tiled=True).reshape(SEQ, 2, 64, D + C_IN)
    attended, logs, attended_full, qkv_kept = call(
        attend_kernel,
        [shape((1024, 128), bf16), Spill((1024, 128), f32), Spill((1024, 128), f32), Copy((SEQ, 192, 128), bf16, 1)],
        Smem(lengths), qkv, flops=8 * 1024 * 1024 * 128, name="attend", mib=32,
    )
    att_recv = to_peers(attended.reshape(SEQ, 64, 128), "seq")
    activations, grad_att_send, gmi, pair_send, pair_own, small_a = call(
        middle_kernel,
        [
            Spill((ROWS, D), bf16), Spill((SEQ, 64, 128), bf16), Spill((ROWS, D), f32),
            shape((ROWS, S_END), bf16), shape((ROWS, O_END), bf16), Spill((16, D), f32),
        ],
        Smem(skip_flag), att_recv, Hbm(hidden), Hbm(cot), Raw(output_weight), Hbm(output_bias), Hbm(middle_gain),
        Hbm(middle_shift), Raw(inner_weight), Hbm(inner_bias), Raw(outer_weight), Hbm(outer_bias), Hbm(final_gain),
        Hbm(final_shift),
        scratch=[
            pltpu.VMEM((ROWS, FF), bf16), pltpu.VMEM((ROWS, FF), f32), pltpu.VMEM((D, D), bf16),
            pltpu.VMEM((D, FF), bf16), pltpu.VMEM((FF, D), bf16), pltpu.VMEM((8, FF), f32), pltpu.VMEM((ROWS, D), f32),
            pltpu.SemaphoreType.DMA((9,)),
        ],
        flops=2 * ROWS * (4 * D * FF + 2 * D * D), name="middle", mib=32,
    )
    swap = [(i, i ^ 1) for i in range(8)]
    pair_got = lax.ppermute(pair_send, "batch", swap)
    grad_att = to_peers(grad_att_send, "seq").reshape(1024, 128)
    (dense,) = call(
        dense_grads_kernel, [Spill((SEQ, 4 * CHUNK, D), bf16, parts=4)], pair_own, pair_send, pair_got,
        flops=2 * 256 * D * 3456, name="dense_grads", mib=24,
    )
    dense, grad_att = lax.optimization_barrier((dense, grad_att))
    dense_part = lax.psum_scatter(dense.reshape(SEQ * 4 * CHUNK, D), "seq", scatter_dimension=0, tiled=True)

    (grad_qkv_send,) = call(
        attend_back_kernel, [Spill((SEQ, 192, 128), bf16)], Smem(lengths), Hbm(qkv_kept), grad_att, Hbm(logs), Hbm(attended_full),
        scratch=[pltpu.VMEM((1024, 128), f32)] * 2 + [pltpu.VMEM((128, Q_BLOCK), f32)], flops=20 * 1024 * 1024 * 128,
        name="attend_back",
    )
    grad_qkv = to_peers(grad_qkv_send, "seq")
    (qkv_rows,) = call(
        head_grads_kernel, [Spill((1024, 384), bf16)], Raw(rows_all), Hbm(grad_qkv_send),
        scratch=[pltpu.VMEM((SEQ, 64, D), bf16), pltpu.SemaphoreType.DMA((1,))], flops=4 * 1024 * D * 384,
        name="head_grads", mib=24,
    )
    frames_normed, frames_high, frames_low = call(
        frames_kernel, [Spill((2048, C_IN), bf16) for _ in range(3)], Raw(rows_all), Hbm(input_gain), Hbm(input_shift),
        scratch=[pltpu.VMEM((SEQ, 2, 64, C_IN), bf16), pltpu.SemaphoreType.DMA((1,))], name="frames", mib=32,
    )
    gmi, qkv_rows, frames_normed = lax.optimization_barrier((gmi, qkv_rows, frames_normed))
    back_send, small_b = call(
        qkv_back_kernel, [shape((SEQ, 32, SW), bf16), Spill((8, D), f32)],
        grad_qkv, Hbm(gmi), Hbm(conv_pre), Hbm(masked), Hbm(encoder_gain), Hbm(qkv_weight),
        scratch=[TRANSPOSE_SCRATCH], flops=2 * ROWS * D * 3 * D, name="qkv_back",
    )
    back_got = to_peers(back_send, "seq")
    back_other = lax.ppermute(back_got, "batch", swap)
    x_other = lax.ppermute(conv_x, "batch", swap)
    (grad_proj,) = call(
        conv_back_kernel, [shape((SEQ, 16, SW), bf16)], Smem(lengths), Hbm(back_got), Hbm(taps),
        scratch=[pltpu.VMEM((BAND, SW), bf16), shifted], flops=conv_flops, name="conv_back", mib=24,
    )
    grad_proj_got = to_peers(grad_proj, "seq")
    (tail,) = call(
        tail_kernel, [shape((1024, 384), bf16)], Hbm(grad_proj), Hbm(small_a), Hbm(small_b),
        Hbm(proj_weight), Hbm(frames_high), Hbm(frames_low), Hbm(frames_normed), Hbm(qkv_rows),
        scratch=[pltpu.VMEM((2048, 128), f32), pltpu.VMEM((3072, 128), f32), pltpu.VMEM((C_IN, 128), f32)],
        flops=6 * 2048 * C_IN * 128, name="tail", mib=32,
    )
    x_other, _ = lax.optimization_barrier((x_other, tail))
    tap_chunks = call(
        conv_weight_kernel, [Spill((GW, D), bf16) for _ in range(4)], Hbm(back_got), Hbm(back_other), Hbm(conv_x),
        Hbm(x_other),
        scratch=[
            pltpu.VMEM((192, BAND), f32), pltpu.VMEM((24, BAND), f32), pltpu.VMEM((192, 128), f32),
            pltpu.VMEM((4, GW, D), bf16), pltpu.VMEM((2, 2, 144, SW), f32),
        ],
        flops=conv_flops, name="conv_grads", mib=32,
    )
    tail, grad_proj_got, *tap_chunks = lax.optimization_barrier((tail, grad_proj_got, *tap_chunks))
    tap_got = []
    for k, piece in enumerate(tap_chunks):
        moves = [
            (b * 16 + g, (g // 2) * 16 + 8 * (g % 2) + 2 * ((b // 2 + k) % 4) + b % 2)
            for b in range(8)
            for g in range(GROUPS)
        ]
        tap_got.append(lax.ppermute(piece, ("batch", "seq"), moves))
    tail_got = to_peers(tail, ("batch", "seq"))
    (tap_own,) = call(conv_sum_kernel, [shape((GW, D), f32)], *[Hbm(x) for x in tap_got], name="conv_sum")
    grad_conv_weight = tap_own.reshape(6, KW, GW).transpose(0, 2, 1)
    dense_own = lax.psum_scatter(dense_part, "batch", scatter_dimension=0, tiled=True, axis_index_groups=Y_GROUPS)
    (grad_feats,) = call(
        feats_back_kernel, [shape((ROWS, C_IN), f32)], grad_proj_got, Hbm(rows_in), Hbm(input_gain), Hbm(proj_weight),
        scratch=[TRANSPOSE_SCRATCH], flops=2 * ROWS * C_IN * D, name="feats_back",
    )
    grad_inner_weight, grad_outer_weight, grad_output_weight = call(
        dense_sum_kernel, [shape((6, FF), f32), shape((24, D), f32), shape((6, D), f32)], Hbm(dense_own),
        name="dense_sum",
    )
    widths = [4, 4] + [6] * 9 + [24] + [6] * 3
    (
        grad_qkv_weight, grad_proj_weight, g_in_g, g_in_s, g_proj_b, g_conv_b, g_enc_g, g_enc_s, g_q_b, g_v_b, g_out_b, g_mid_g, g_mid_s,
        g_inner_b, g_outer_b, g_fin_g, g_fin_s,
    ) = call(
        tail_sum_kernel, [shape((6, 3 * D), f32), shape((4, D), f32)] + [shape((w,), f32) for w in widths],
        tail_got.reshape(128, 8, 384),
        name="tail_sum",
    )
    return (
        activations.reshape(2, 64, D), grad_feats.reshape(2, 64, C_IN), g_in_g, g_in_s, grad_proj_weight, g_proj_b,
        grad_conv_weight, g_conv_b, g_enc_g, g_enc_s, grad_qkv_weight, g_q_b, g_v_b, grad_output_weight, g_out_b,
        g_mid_g, g_mid_s, grad_inner_weight, g_inner_b, grad_outer_weight, g_outer_b, g_fin_g, g_fin_s,
    )


def solution(mesh):
    split = P("batch", "seq", None)
    both = ("batch", "seq")
    placed = (split, P("batch"), P("batch"), split) + (P(),) * 21
    row, matrix = P(both), P(both, None)
    return jax.shard_map(
        local,
        mesh=mesh,
        in_specs=placed,
        out_specs=(
            split, split, row, row, matrix, row, P(both, None, None), row, row, row, matrix, row, row, matrix, row,
            row, row, matrix, row, matrix, row, row, row,
        ),
        check_vma=False,
    )
```

profile of v0, /device:TPU:1, one launch (start us, length us, event | category | flops | bytes accessed | tf_op | source)
XLA Modules:
  0.0 234.7 jit_solution(7805675737611863543)
XLA Ops:
  7.8 3.1 %project.1 = (f32[128,768]{1,0:T(8,128)}, bf16[16,16,384]{2,1,0:T(8,128)(2,1)}) custom-call(s32[2]{0:T(128)S(1)} %copy-done.2, bf16[128,512]{1,0:T(8,128)(2,1)} %bitcast.16, bf16[512]{0:T(512)(128)(2,1)} %refs_2_.7, bf16[512]{0:T(512)(128)(2,1)} %refs_2_.6, bf16[512,768]{1,0:T(8,128)(2,1)} %refs_3_.7, bf16[768]{0:T(1024)(128)(2,1)} %refs_5_.4), custom_call_target="tpu_custom_call" | custom-call | flops 100663296 | bytes 1510920 | tf_op jit(solution)/shard_map/project/pallas_call | solution.py:228
  11.0 8.4 %all-to-all-start = ((bf16[16,16,384]{2,1,0:T(8,128)(2,1)}), bf16[16,16,384]{2,1,0:T(8,128)(2,1)S(1)}, u32[]{:S(2)}, u32[]{:S(2)}) async-start(bf16[16,16,384]{2,1,0:T(8,128)(2,1)} %get-tuple-element.82), calls=%async_computation | async-start | bytes 393216 | tf_op jit(solution)/shard_map/all_to_all | solution.py:807
  21.4 3.6 %reshape.81.refs_1_.refs_2_ = bf16[48,6144]{1,0:T(8,128)(2,1)} reshape(bf16[48,128,48]{2,1,0:T(8,128)(2,1)S(1)} %copy.50) | data formatting | bytes 1179648 | tf_op jit(solution)/shard_map/reshape | solution.py:830
  26.6 3.4 %conv.1 = (bf16[16,16,384]{2,1,0:T(8,128)(2,1)S(1)}, bf16[16,16,384]{2,1,0:T(8,128)(2,1)}) custom-call(bf16[16,16,384]{2,1,0:T(8,128)(2,1)S(1)} %all-to-all-done.refs_0_, bf16[48,6144]{1,0:T(8,128)(2,1)} %reshape.81.refs_1_.refs_2_), custom_call_target="tpu_custom_call" | custom-call | flops 1283457024 | bytes 1179648 | tf_op jit(solution)/shard_map/conv/pallas_call | solution.py:228
  30.0 11.9 %all_to_all.49.refs_0_ = bf16[16,16,384]{2,1,0:T(8,128)(2,1)S(1)} all-to-all(bf16[16,16,384]{2,1,0:T(8,128)(2,1)S(1)} %get-tuple-element.83), channel_id=1, replica_groups=mesh['batch'=8,'seq'=16] {'seq'}, dimensions={0} | all-to-all | bytes 393216 | tf_op jit(solution)/shard_map/all_to_all | solution.py:807
  41.9 4.0 %qkv.1 = (f32[128,768]{1,0:T(8,128)}, f32[128,768]{1,0:T(8,128)}, bf16[16,192,128]{2,1,0:T(8,128)(2,1)}, bf16[128,1280]{1,0:T(8,128)(2,1)}) custom-call(bf16[16,16,384]{2,1,0:T(8,128)(2,1)S(1)} %all_to_all.49.refs_0_, f32[128,768]{1,0:T(8,128)} %get-tuple-element.84.refs_1_.refs_3_, bf16[768]{0:T(1024)(128)(2,1)} %refs_2_.5, bf16[768]{0:T(1024)(128)(2,1)} %refs_4_.7, ...), custom_call_target="tpu_custom_call" | custom-call | flops 452984832 | bytes 6168064 | tf_op jit(solution)/shard_map/qkv/pallas_call | solution.py:228
  45.9 14.7 %all_to_all.50.refs_1_ = bf16[16,192,128]{2,1,0:T(8,128)(2,1)S(1)} all-to-all(bf16[16,192,128]{2,1,0:T(8,128)(2,1)} %get-tuple-element.85), channel_id=1, replica_groups=mesh['batch'=8,'seq'=16] {'seq'}, dimensions={0} | all-to-all | bytes 1572864 | tf_op jit(solution)/shard_map/all_to_all | solution.py:807
  60.6 5.9 %attend.1 = (bf16[1024,128]{1,0:T(8,128)(2,1)}, f32[1024,128]{1,0:T(8,128)}, f32[1024,128]{1,0:T(8,128)}, bf16[16,192,128]{2,1,0:T(8,128)(2,1)}) custom-call(s32[2]{0:T(128)S(1)} %copy-done.3, bf16[16,192,128]{2,1,0:T(8,128)(2,1)S(1)} %all_to_all.50.refs_1_), custom_call_target="tpu_custom_call" | custom-call | flops 1073741824 | bytes 2883592 | tf_op jit(solution)/shard_map/attend/pallas_call | solution.py:228
  66.5 4.1 %all-to-all-start.3 = ((bf16[16,64,128]{2,1,0:T(8,128)(2,1)}), bf16[16,64,128]{2,1,0:T(8,128)(2,1)S(1)}, u32[]{:S(2)}, u32[]{:S(2)}) async-start(bf16[16,64,128]{2,1,0:T(8,128)(2,1)} %bitcast.2), calls=%async_computation.3 | async-start | bytes 524288 | tf_op jit(solution)/shard_map/all_to_all | solution.py:807
  71.2 6.7 %all-to-all-done.3.refs_1_ = bf16[16,64,128]{2,1,0:T(8,128)(2,1)S(1)} async-done(((bf16[16,64,128]{2,1,0:T(8,128)(2,1)}), bf16[16,64,128]{2,1,0:T(8,128)(2,1)S(1)}, u32[]{:S(2)}, u32[]{:S(2)}) %all-to-all-start.3) | async-done | bytes 262176 | tf_op jit(solution)/shard_map/all_to_all | solution.py:807
  77.9 14.8 %middle.1 = (bf16[128,768]{1,0:T(8,128)(2,1)}, bf16[16,64,128]{2,1,0:T(8,128)(2,1)}, f32[128,768]{1,0:T(8,128)}, bf16[128,6912]{1,0:T(8,128)(2,1)S(1)}, bf16[128...) custom-call(s32[1]{0:T(128)S(6)} %copy.52.refs_0_, bf16[16,64,128]{2,1,0:T(8,128)(2,1)S(1)} %all-to-all-done.3.refs_1_, ...), custom_call_target="tpu_custom_call" | custom-call | flops 2717908992 | bytes 14744580 | tf_op jit(solution)/shard_map/middle/pallas_call | solution.py:228
  93.6 6.3 %collective-permute-start = (bf16[128,6912]{1,0:T(8,128)(2,1)S(1)}, bf16[128,6912]{1,0:T(8,128)(2,1)S(1)}, u32[]{:S(2)}, u32[]{:S(2)}) collective-permute-start(bf16[128,6912]{1,0:T(8,128)(2,1)S(1)} %get-tuple-element.91.refs_1_), channel_id=1, source_target_pairs={{0,16},{16,0},{32,48},{48,32},{64,80},{80,64},{96,112},{112,96},{1... | collective-permute-start | bytes 5308424 | tf_op jit(solution)/shard_map/ppermute | solution.py:873
  99.9 4.2 %all-to-all-start.4 = ((bf16[16,64,128]{2,1,0:T(8,128)(2,1)}), bf16[16,64,128]{2,1,0:T(8,128)(2,1)}, u32[]{:S(2)}, u32[]{:S(2)}) async-start(bf16[16,64,128]{2,1,0:T(8,128)(2,1)} %get-tuple-element.92), calls=%async_computation.4 | async-start | bytes 524288 | tf_op jit(solution)/shard_map/all_to_all | solution.py:807
  105.3 4.7 %dense_grads.1 = bf16[16,224,768]{2,1,0:T(8,128)(2,1)} custom-call(bf16[128,2304]{1,0:T(8,128)(2,1)S(1)} %copy-done.1, bf16[128,6912]{1,0:T(8,128)(2,1)S(1)} %get-tuple-element.91.refs_1_, bf16[128,6912]{1,0:T(8,128)(2,1)S(1)} %collective-permute-done.refs_2_), custom_call_target="tpu_custom_call" | custom-call | flops 1358954496 | bytes 9633792 | tf_op jit(solution)/shard_map/dense_grads/pallas_call | solution.py:228
  109.9 2.2 all-to-all-done.4
  112.1 10.8 %attend_back.1.refs_1_ = bf16[16,192,128]{2,1,0:T(8,128)(2,1)} custom-call(s32[2]{0:T(128)S(1)} %copy-done.3, bf16[16,192,128]{2,1,0:T(8,128)(2,1)} %get-tuple-element.89.refs_1_, bf16[1024,128]{1,0:T(8,128)(2,1)} %bitcast.5.refs_2_, f32[1024,128]{1,0:T(8,128)} %get-tuple-element.94.refs_3_, f32[1024,128]{1,0:T(8,128)} %get-tuple-element.95.refs_4_), custom_call_target="tpu_custom_call" | custom-call | flops 2684354560 | bytes 2883592 | tf_op jit(solution)/shard_map/attend_back/pallas_call | solution.py:228
  122.9 4.4 %all-to-all-start.5 = ((bf16[16,192,128]{2,1,0:T(8,128)(2,1)}), bf16[16,192,128]{2,1,0:T(8,128)(2,1)S(1)}, u32[]{:S(2)}, u32[]{:S(2)}) async-start(bf16[16,192,128]{2,1,0:T(8,128)(2,1)} %attend_back.1.refs_1_), calls=%async_computation.5 | async-start | bytes 1572864 | tf_op jit(solution)/shard_map/all_to_all | solution.py:807
  127.3 8.1 %frames.1 = (bf16[2048,512]{1,0:T(8,128)(2,1)}, bf16[2048,512]{1,0:T(8,128)(2,1)}, bf16[2048,512]{1,0:T(8,128)(2,1)}) custom-call(bf16[16,2,64,1280]{3,2,1,0:T(8,128)(2,1)} %bitcast.13, bf16[512]{0:T(512)(128)(2,1)} %refs_2_.7, bf16[512]{0:T(512)(128)(2,1)} %refs_2_.6), custom_call_target="tpu_custom_call" | custom-call | bytes 11536384 | tf_op jit(solution)/shard_map/frames/pallas_call | solution.py:228
  135.5 5.1 %head_grads.1.refs_7_ = bf16[1024,384]{1,0:T(8,128)(2,1)} custom-call(bf16[16,2,64,1280]{3,2,1,0:T(8,128)(2,1)} %bitcast.14, bf16[16,192,128]{2,1,0:T(8,128)(2,1)} %attend_back.1.refs_1_), custom_call_target="tpu_custom_call" | custom-call | flops 1207959552 | bytes 6815744 | tf_op jit(solution)/shard_map/head_grads/pallas_call | solution.py:228
  140.6 4.1 %all-to-all-done.5.refs_0_ = bf16[16,192,128]{2,1,0:T(8,128)(2,1)S(1)} async-done(((bf16[16,192,128]{2,1,0:T(8,128)(2,1)}), bf16[16,192,128]{2,1,0:T(8,128)(2,1)S(1)}, u32[]{:S(2)}, u32[]{:S(2)}) %all-to-all-start.5) | async-done | bytes 786464 | tf_op jit(solution)/shard_map/all_to_all | solution.py:807
  144.7 4.9 %qkv_back.1 = (bf16[16,32,384]{2,1,0:T(8,128)(2,1)S(1)}, f32[8,768]{1,0:T(8,128)}) custom-call(bf16[16,192,128]{2,1,0:T(8,128)(2,1)S(1)} %all-to-all-done.5.refs_0_, f32[128,768]{1,0:T(8,128)} %get-tuple-element.99.refs_1_, f32[128,768]{1,0:T(8,128)} %get-tuple-element.100.refs_2_, f32[128,768]{1,0:T(8,128)} %get-tuple-element.84.refs_1_.refs_3_, ...), custom_call_target="tpu_custom_call" | custom-call | flops 452984832 | bytes 5924352 | tf_op jit(solution)/shard_map/qkv_back/pallas_call | solution.py:228
  149.6 14.4 %all_to_all.51.refs_1_.refs_0_ = bf16[16,32,384]{2,1,0:T(8,128)(2,1)S(1)} all-to-all(bf16[16,32,384]{2,1,0:T(8,128)(2,1)S(1)} %get-tuple-element.101), channel_id=1, replica_groups=mesh['batch'=8,'seq'=16] {'seq'}, dimensions={0} | all-to-all | bytes 786432 | tf_op jit(solution)/shard_map/all_to_all | solution.py:807
  164.0 2.3 collective-permute-start.1
  166.4 5.1 %conv_back.1.refs_0_ = bf16[16,16,384]{2,1,0:T(8,128)(2,1)} custom-call(s32[2]{0:T(128)S(1)} %copy-done.3, bf16[16,32,384]{2,1,0:T(8,128)(2,1)} %copy-done.4, bf16[48,6144]{1,0:T(8,128)(2,1)} %reshape.81.refs_1_.refs_2_), custom_call_target="tpu_custom_call" | custom-call | flops 1283457024 | bytes 1179656 | tf_op jit(solution)/shard_map/conv_back/pallas_call | solution.py:228
  171.5 3.8 %all-to-all-start.7 = ((bf16[16,16,384]{2,1,0:T(8,128)(2,1)}), bf16[16,16,384]{2,1,0:T(8,128)(2,1)S(1)}, u32[]{:S(2)}, u32[]{:S(2)}) async-start(bf16[16,16,384]{2,1,0:T(8,128)(2,1)} %conv_back.1.refs_0_), calls=%async_computation.7 | async-start | bytes 393216 | tf_op jit(solution)/shard_map/all_to_all | solution.py:807
  175.3 6.1 %tail.1 = bf16[1024,384]{1,0:T(8,128)(2,1)} custom-call(bf16[16,16,384]{2,1,0:T(8,128)(2,1)} %conv_back.1.refs_0_, f32[16,768]{1,0:T(8,128)} %get-tuple-element.102.refs_1_, f32[8,768]{1,0:T(8,128)} %get-tuple-element.103.refs_2_, bf16[512,768]{1,0:T(8,128)(2,1)} %refs_3_.7, bf16[2048,512]{1,0:T(8,128)(2,1)} %get-tuple-element.104.refs_4_, ...), custom_call_target="tpu_custom_call" | custom-call | flops 805306368 | bytes 8921088 | tf_op jit(solution)/shard_map/tail/pallas_call | solution.py:228
  182.9 4.5 %conv_grads.1 = (bf16[48,768]{1,0:T(8,128)(2,1)}, bf16[48,768]{1,0:T(8,128)(2,1)}, bf16[48,768]{1,0:T(8,128)(2,1)}, bf16[48,768]{1,0:T(8,128)(2,1)}) custom-call(bf16[16,32,384]{2,1,0:T(8,128)(2,1)} %copy-done.4, bf16[16,32,384]{2,1,0:T(8,128)(2,1)} %copy-done.9, bf16[16,16,384]{2,1,0:T(8,128)(2,1)} %get-tuple-element.108.refs_2_, ...), custom_call_target="tpu_custom_call" | custom-call | flops 1283457024 | bytes 1474560 | tf_op jit(solution)/shard_map/conv_grads/pallas_call | solution.py:228
  187.4 11.2 %all-to-all-start.8 = ((bf16[128,8,384]{2,1,0:T(8,128)(2,1)}), bf16[128,8,384]{2,1,0:T(8,128)(2,1)S(1)}, u32[]{:S(2)}, u32[]{:S(2)}) async-start(bf16[128,8,384]{2,1,0:T(8,128)(2,1)} %bitcast.8), calls=%async_computation.8 | async-start | bytes 1572864 | tf_op jit(solution)/shard_map/all_to_all | solution.py:807
  199.3 3.7 %collective-permute-start.3 = (bf16[48,768]{1,0:T(8,128)(2,1)}, bf16[48,768]{1,0:T(8,128)(2,1)S(1)}, u32[]{:S(2)}, u32[]{:S(2)}) collective-permute-start(bf16[48,768]{1,0:T(8,128)(2,1)} %get-tuple-element.120), channel_id=1, source_target_pairs={{0,0},{1,8},{2,16},{3,24},{4,32},{5,40},{6,48},{7,56},{8,64},{9,72... | collective-permute-start | bytes 221192 | tf_op jit(solution)/shard_map/ppermute | solution.py:935
  202.9 5.7 %collective-permute-start.4 = (bf16[48,768]{1,0:T(8,128)(2,1)}, bf16[48,768]{1,0:T(8,128)(2,1)S(1)}, u32[]{:S(2)}, u32[]{:S(2)}) collective-permute-start(bf16[48,768]{1,0:T(8,128)(2,1)} %get-tuple-element.121), channel_id=1, source_target_pairs={{0,2},{1,10},{2,18},{3,26},{4,34},{5,42},{6,50},{7,58},{8,66},{9,7... | collective-permute-start | bytes 221192 | tf_op jit(solution)/shard_map/ppermute | solution.py:935
  210.7 9.0 %collective-permute-start.6 = (bf16[48,768]{1,0:T(8,128)(2,1)}, bf16[48,768]{1,0:T(8,128)(2,1)S(1)}, u32[]{:S(2)}, u32[]{:S(2)}) collective-permute-start(bf16[48,768]{1,0:T(8,128)(2,1)} %get-tuple-element.123), channel_id=1, source_target_pairs={{0,6},{1,14},{2,22},{3,30},{4,38},{5,46},{6,54},{7,62},{8,70},{9,7... | collective-permute-start | bytes 221192 | tf_op jit(solution)/shard_map/ppermute | solution.py:935
  219.7 2.6 %feats_back.1 = f32[128,512]{1,0:T(8,128)} custom-call(bf16[16,16,384]{2,1,0:T(8,128)(2,1)S(1)} %all-to-all-done.7.refs_0_, bf16[128,512]{1,0:T(8,128)(2,1)} %bitcast.18, bf16[512]{0:T(512)(128)(2,1)} %refs_2_.7, bf16[512,768]{1,0:T(8,128)(2,1)} %refs_3_.7), custom_call_target="tpu_custom_call" | custom-call | flops 100663296 | bytes 1377280 | tf_op jit(solution)/shard_map/feats_back/pallas_call | solution.py:228
  (52 shorter events, 16.2 us)
Async XLA Ops:
  7.2 0.7 copy-start.2
  11.0 15.6 %all-to-all-start = ((bf16[16,16,384]{2,1,0:T(8,128)(2,1)}), bf16[16,16,384]{2,1,0:T(8,128)(2,1)S(1)}, u32[]{:S(2)}, u32[]{:S(2)}) async-start(bf16[16,16,384]{2,1,0:T(8,128)(2,1)} %get-tuple-element.82), calls=%async_computation | async-start | bytes 393216 | tf_op jit(solution)/shard_map/all_to_all | solution.py:807
  19.4 107.9 %all-gather.2.cloned.1.call-start = ((), (), s32[]{:S(2)}) async-start(), calls=%async_computation.11 | async-start | bytes 5570560 | tf_op jit(solution)/shard_map/all_gather | solution.py:849
  30.0 30.6 %copy-start.3 = (s32[2]{0:T(128)S(1)}, s32[2]{0:T(128)}, u32[]{:S(2)}) copy-start(s32[2]{0:T(128)} %refs_0_.8) | copy-start | bytes 28
  66.5 11.4 %all-to-all-start.3 = ((bf16[16,64,128]{2,1,0:T(8,128)(2,1)}), bf16[16,64,128]{2,1,0:T(8,128)(2,1)S(1)}, u32[]{:S(2)}, u32[]{:S(2)}) async-start(bf16[16,64,128]{2,1,0:T(8,128)(2,1)} %bitcast.2), calls=%async_computation.3 | async-start | bytes 524288 | tf_op jit(solution)/shard_map/all_to_all | solution.py:807
  92.8 0.8 copy-start
  93.6 10.6 %collective-permute-start = (bf16[128,6912]{1,0:T(8,128)(2,1)S(1)}, bf16[128,6912]{1,0:T(8,128)(2,1)S(1)}, u32[]{:S(2)}, u32[]{:S(2)}) collective-permute-start(bf16[128,6912]{1,0:T(8,128)(2,1)S(1)} %get-tuple-element.91.refs_1_), channel_id=1, source_target_pairs={{0,16},{16,0},{32,48},{48,32},{64,80},{80,64},{96,112},{112,96},{1... | collective-permute-start | bytes 5308424 | tf_op jit(solution)/shard_map/ppermute | solution.py:873
  99.9 12.2 %all-to-all-start.4 = ((bf16[16,64,128]{2,1,0:T(8,128)(2,1)}), bf16[16,64,128]{2,1,0:T(8,128)(2,1)}, u32[]{:S(2)}, u32[]{:S(2)}) async-start(bf16[16,64,128]{2,1,0:T(8,128)(2,1)} %get-tuple-element.92), calls=%async_computation.4 | async-start | bytes 524288 | tf_op jit(solution)/shard_map/all_to_all | solution.py:807
  104.1 94.5 %reduce-scatter.3.cloned.1.call-start = ((), (), s32[]{:S(2)}) async-start(), calls=%async_computation.12 | async-start | bytes 5849088 | tf_op jit(solution)/shard_map/reduce_scatter | solution.py:880
  104.2 1.1 copy-start.1
  122.9 21.7 %all-to-all-start.5 = ((bf16[16,192,128]{2,1,0:T(8,128)(2,1)}), bf16[16,192,128]{2,1,0:T(8,128)(2,1)S(1)}, u32[]{:S(2)}, u32[]{:S(2)}) async-start(bf16[16,192,128]{2,1,0:T(8,128)(2,1)} %attend_back.1.refs_1_), calls=%async_computation.5 | async-start | bytes 1572864 | tf_op jit(solution)/shard_map/all_to_all | solution.py:807
  140.6 25.7 %copy-start.10 = (bf16[16,16,384]{2,1,0:T(8,128)(2,1)S(1)}, bf16[16,16,384]{2,1,0:T(8,128)(2,1)}, u32[]{:S(2)}) copy-start(bf16[16,16,384]{2,1,0:T(8,128)(2,1)} %get-tuple-element.108.refs_2_) | copy-start | bytes 589828
  164.0 2.4 %copy-start.4 = (bf16[16,32,384]{2,1,0:T(8,128)(2,1)}, bf16[16,32,384]{2,1,0:T(8,128)(2,1)S(1)}, u32[]{:S(2)}) copy-start(bf16[16,32,384]{2,1,0:T(8,128)(2,1)S(1)} %all_to_all.51.refs_1_.refs_0_) | copy-start | bytes 1179652
  164.0 17.5 %collective-permute-start.1 = (bf16[16,32,384]{2,1,0:T(8,128)(2,1)S(1)}, bf16[16,32,384]{2,1,0:T(8,128)(2,1)S(1)}, u32[]{:S(2)}, u32[]{:S(2)}) collective-permute-start(bf16[16,32,384]{2,1,0:T(8,128)(2,1)S(1)} %all_to_all.51.refs_1_.refs_0_), channel_id=1, source_target_pairs={{0,16},{16,0},{32,48},{48,32},{64,80},{80,64},{96,112},{112,96},{1... | collective-permute-start | bytes 1179656 | tf_op jit(solution)/shard_map/ppermute | solution.py:904
  166.3 15.1 %collective-permute-start.2 = (bf16[16,16,384]{2,1,0:T(8,128)(2,1)S(1)}, bf16[16,16,384]{2,1,0:T(8,128)(2,1)S(1)}, u32[]{:S(2)}, u32[]{:S(2)}) collective-permute-start(bf16[16,16,384]{2,1,0:T(8,128)(2,1)S(1)} %copy-done.10), channel_id=1, source_target_pairs={{0,16},{16,0},{32,48},{48,32},{64,80},{80,64},{96,112},{112,96},{1... | collective-permute-start | bytes 589832 | tf_op jit(solution)/shard_map/ppermute | solution.py:905
  171.5 15.9 %all-to-all-start.7 = ((bf16[16,16,384]{2,1,0:T(8,128)(2,1)}), bf16[16,16,384]{2,1,0:T(8,128)(2,1)S(1)}, u32[]{:S(2)}, u32[]{:S(2)}) async-start(bf16[16,16,384]{2,1,0:T(8,128)(2,1)} %conv_back.1.refs_0_), calls=%async_computation.7 | async-start | bytes 393216 | tf_op jit(solution)/shard_map/all_to_all | solution.py:807
  181.4 0.7 copy-start.11
  182.1 0.8 copy-start.9
  187.4 38.3 %all-to-all-start.8 = ((bf16[128,8,384]{2,1,0:T(8,128)(2,1)}), bf16[128,8,384]{2,1,0:T(8,128)(2,1)S(1)}, u32[]{:S(2)}, u32[]{:S(2)}) async-start(bf16[128,8,384]{2,1,0:T(8,128)(2,1)} %bitcast.8), calls=%async_computation.8 | async-start | bytes 1572864 | tf_op jit(solution)/shard_map/all_to_all | solution.py:807
  198.5 28.1 %reduce-scatter.5.cloned.1.call-start = ((), (), s32[]{:S(2)}) async-start(), calls=%async_computation.13 | async-start | bytes 430080 | tf_op jit(solution)/shard_map/reduce_scatter | solution.py:939
  199.3 23.1 %collective-permute-start.3 = (bf16[48,768]{1,0:T(8,128)(2,1)}, bf16[48,768]{1,0:T(8,128)(2,1)S(1)}, u32[]{:S(2)}, u32[]{:S(2)}) collective-permute-start(bf16[48,768]{1,0:T(8,128)(2,1)} %get-tuple-element.120), channel_id=1, source_target_pairs={{0,0},{1,8},{2,16},{3,24},{4,32},{5,40},{6,48},{7,56},{8,64},{9,72... | collective-permute-start | bytes 221192 | tf_op jit(solution)/shard_map/ppermute | solution.py:935
  202.9 19.4 %collective-permute-start.4 = (bf16[48,768]{1,0:T(8,128)(2,1)}, bf16[48,768]{1,0:T(8,128)(2,1)S(1)}, u32[]{:S(2)}, u32[]{:S(2)}) collective-permute-start(bf16[48,768]{1,0:T(8,128)(2,1)} %get-tuple-element.121), channel_id=1, source_target_pairs={{0,2},{1,10},{2,18},{3,26},{4,34},{5,42},{6,50},{7,58},{8,66},{9,7... | collective-permute-start | bytes 221192 | tf_op jit(solution)/shard_map/ppermute | solution.py:935
  208.7 13.7 %collective-permute-start.5 = (bf16[48,768]{1,0:T(8,128)(2,1)}, bf16[48,768]{1,0:T(8,128)(2,1)S(1)}, u32[]{:S(2)}, u32[]{:S(2)}) collective-permute-start(bf16[48,768]{1,0:T(8,128)(2,1)} %get-tuple-element.122), channel_id=1, source_target_pairs={{0,4},{1,12},{2,20},{3,28},{4,36},{5,44},{6,52},{7,60},{8,68},{9,7... | collective-permute-start | bytes 221192 | tf_op jit(solution)/shard_map/ppermute | solution.py:935
  210.7 11.7 %collective-permute-start.6 = (bf16[48,768]{1,0:T(8,128)(2,1)}, bf16[48,768]{1,0:T(8,128)(2,1)S(1)}, u32[]{:S(2)}, u32[]{:S(2)}) collective-permute-start(bf16[48,768]{1,0:T(8,128)(2,1)} %get-tuple-element.123), channel_id=1, source_target_pairs={{0,6},{1,14},{2,22},{3,30},{4,38},{5,46},{6,54},{7,62},{8,70},{9,7... | collective-permute-start | bytes 221192 | tf_op jit(solution)/shard_map/ppermute | solution.py:935
  222.3 0.6 copy-start.5
  222.4 0.6 copy-start.6
  222.4 0.6 copy-start.7
  223.0 0.6 copy-start.8
Sparse Core Ops, SparseCore 0:
  46.0 58.8 all-gather.1
  112.2 85.8 reduce-scatter.2
  201.7 24.3 reduce-scatter.4
where the time goes:
time: 239 us; the launch traced here: 235 us
  Pallas kernels  86.6 us (36%)
  starting transfers between devices  65.4 us (27%)
  blocking collectives  40.9 us (17%)
  waiting for transfers between devices  15.2 us (6%)
  between operations  14.8 us (6%)
  local copies, waits for them, and re-layouts  11.8 us (5%)
    pallas_call x17, Pallas kernels, call(): pl.pallas_call(wrapped, out_shape=[pltpu.HBM(o.struct.shape, o.struct.dty...  86.6 us
    all_to_all x3, blocking collectives, to_peers(): return lax.all_to_all(x, axis, 0, 0, tiled=True, axis_index_groups=groups)  40.9 us
    all_to_all x6, starting transfers between devices, to_peers(): return lax.all_to_all(x, axis, 0, 0, tiled=True, axis_index_groups=groups)  36.1 us
    ppermute x4, starting transfers between devices, local(): tap_got.append(lax.ppermute(piece, ('batch', 'seq'), moves))  20.4 us
    all_to_all x6, waiting for transfers between devices, to_peers(): return lax.all_to_all(x, axis, 0, 0, tiled=True, axis_index_groups=groups)  14.5 us
    ppermute x1, starting transfers between devices, local(): pair_got = lax.ppermute(pair_send, 'batch', swap)  6.34 us
    unnamed x25, local copies, waits for them, and re-layouts  6.03 us
  transfers between devices with their start and end apart: 16, of which 4 were waited for; matrix products, arithmetic and copies ran while one was open for 3% of the time, Pallas kernels for 32%

commit v1 on v0

--- a/solution.py
+++ b/solution.py
@@ -264,12 +264,12 @@
     return lax.axis_index("batch") & 1
 
 
-def project_kernel(lengths, feats, gain, shift, weight, bias, masked_out, send_out, scratch):
+def project_kernel(feats, gain, shift, weight, bias, projected_out, send_out, scratch):
     xhat, _ = stats(feats()[...].astype(f32))
     normed = (xhat * vec(gain) + vec(shift)).astype(bf16)
-    masked = (nn(normed, weight()[...]) + vec(bias)) * live_rows(lengths)
-    masked_out.put(masked)
-    for g, x in enumerate(rows_to_groups(masked, scratch)):
+    projected = nn(normed, weight()[...]) + vec(bias)
+    projected_out.put(projected)
+    for g, x in enumerate(rows_to_groups(projected, scratch)):
         send_out[g] = x.astype(bf16)
 
 
@@ -297,11 +297,20 @@
     return jnp.concatenate([x[u * 128 + p * 8 : u * 128 + p * 8 + 8] for u in range(2)], axis=0)
 
 
-def conv_kernel(x, taps, out, x_out, w, scratch):
+def group_live(ref, p):
+    row, f = iota((16, SW), 0), int_div(iota((1, SW), 1), GW)
+    return p * 64 + (row & 7) * SUPER + f < jnp.where(row < 8, ref[0], ref[1])
+
+
+def conv_kernel(lengths, x, taps, out, x_out, w, scratch):
+    ref = lengths()
+    masked = [jnp.where(group_live(ref, p), x[p].astype(f32), 0.0) for p in range(SEQ)]
+    for p in range(SEQ):
+        x_out.ref[p] = masked[p].astype(bf16)
     x_out.flush()
+    padded(masked, scratch)
     for f, rows in enumerate(band_rows(taps())):
         w[f * GW : (f + 1) * GW, :] = rows
-    padded([x[p].astype(f32) for p in range(SEQ)], scratch)
     res = nt(windows(scratch, range(TAP_BLOCKS)), w[...])
     for p in range(SEQ):
         out[p] = by_seq(res, p).astype(bf16)
@@ -317,13 +326,10 @@
     got = got_in()
     padded([got[p, :16, :].astype(f32) for p in range(SEQ)], scratch)
     res = nn(windows(scratch, range(16, -1, -1)), w[...])
-    row, f = iota((16, SW), 0), int_div(iota((1, SW), 1), GW)
     ref = lengths()
-    length = jnp.where(row < 8, ref[0], ref[1])
     for p in range(SEQ):
         total = by_seq(res, p) + got[p, 16:, :].astype(f32)
-        live = p * 64 + (row & 7) * SUPER + f < length
-        out[p] = jnp.where(live, total, 0.0).astype(bf16)
+        out[p] = jnp.where(group_live(ref, p), total, 0.0).astype(bf16)
 
 
 def conv_weight_kernel(got_in, other_in, x_in, x_other, *rest):
@@ -371,12 +377,14 @@
 
 
 def qkv_kernel(
-    conv, masked, conv_bias, gain, shift, weight, query_bias, value_bias, feats,
-    pre_out, hidden_out, send_out, rows_out, scratch,
+    lengths, conv, projected, conv_bias, gain, shift, weight_in, query_bias, value_bias, feats,
+    pre_out, hidden_out, send_out, rows_out, scratch, weight, sems,
 ):
+    cols = [slice(block * D, (block + 1) * D) for block in (1, 2, 0)]
+    copies = fetch(sems, *[(weight_in.at[:, c], weight.at[:, c]) for c in cols])
     pre = groups_to_rows(conv, scratch) + vec(conv_bias)
     pre_out.put(pre)
-    xhat, _ = stats(masked()[...] + gelu(pre))
+    xhat, _ = stats(projected()[...] * live_rows(lengths) + gelu(pre))
     hidden = xhat * vec(gain) + vec(shift)
     hidden_out.put(hidden)
     hidden_b = hidden.astype(bf16)
@@ -385,8 +393,9 @@
     rows_out.flush()
     zero = jnp.zeros((1, D), f32)
     send = send_out.ref
-    for slot, (block, bias) in enumerate(((1, zero), (2, vec(value_bias)), (0, vec(query_bias)))):
-        part = (nn(hidden_b, weight()[:, block * D : (block + 1) * D]) + bias).astype(bf16)
+    for slot, bias in enumerate((zero, vec(value_bias), vec(query_bias))):
+        copies[slot].wait()
+        part = (nn(hidden_b, weight[:, cols[slot]]) + bias).astype(bf16)
         for u in range(2):
             for pair in range(PAIRS):
                 send[u * PAIRS + pair, slot * 64 : (slot + 1) * 64, :] = part[
@@ -672,11 +681,11 @@
 
 
 def qkv_back_kernel(
-    recv, gmi, pre_in, masked, gain_in, weight, send_out, small_out, scratch
+    lengths, recv, gmi, pre_in, projected, gain_in, weight, send_out, small_out, scratch
 ):
     pre = pre_in()[...]
     gain = vec(gain_in)
-    xhat, r = stats(masked()[...] + gelu(pre))
+    xhat, r = stats(projected()[...] * live_rows(lengths) + gelu(pre))
     grad_hidden = gmi()[...]
     sums = []
     for slot in range(3):
@@ -819,10 +828,10 @@
     rows_in = feats.reshape(ROWS, C_IN)
     cot = cotangent.reshape(ROWS, D)
 
-    masked, conv_send = call(
+    projected, conv_send = call(
         project_kernel,
         [Spill((ROWS, D), f32), shape((GROUPS, 16, SW), bf16)],
-        Smem(lengths), Hbm(rows_in), Hbm(input_gain), Hbm(input_shift), Hbm(proj_weight), Hbm(proj_bias),
+        Hbm(rows_in), Hbm(input_gain), Hbm(input_shift), Hbm(proj_weight), Hbm(proj_bias),
         flops=2 * ROWS * C_IN * D, name="project", scratch=[TRANSPOSE_SCRATCH],
     )
     conv_x = to_peers(conv_send, "seq")
@@ -831,7 +840,7 @@
     shifted = pltpu.VMEM((2, 144, SW), f32)
     conv_flops = 2 * 256 * SW * BAND
     conv_y, conv_x = call(
-        conv_kernel, [shape((SEQ, 16, SW), bf16), Copy((SEQ, 16, SW), bf16, 0)], conv_x, Hbm(taps),
+        conv_kernel, [shape((SEQ, 16, SW), bf16), Spill((SEQ, 16, SW), bf16)], Smem(lengths), conv_x, Hbm(taps),
         scratch=[pltpu.VMEM((SW, BAND), bf16), shifted],
         flops=conv_flops, name="conv", mib=24,
     )
@@ -842,8 +851,10 @@
             Spill((ROWS, D), f32), Spill((ROWS, D), f32), Spill((SEQ, 192, 128), bf16, parts=3),
             Spill((ROWS, D + C_IN), bf16),
         ],
-        conv_back, Hbm(masked), Hbm(conv_bias), Hbm(encoder_gain), Hbm(encoder_shift), Hbm(qkv_weight), Hbm(query_bias),
-        Hbm(value_bias), Hbm(rows_in), flops=2 * ROWS * D * 3 * D, name="qkv", scratch=[TRANSPOSE_SCRATCH],
+        Smem(lengths), conv_back, Hbm(projected), Hbm(conv_bias), Hbm(encoder_gain), Hbm(encoder_shift), Raw(qkv_weight),
+        Hbm(query_bias),
+        Hbm(value_bias), Hbm(rows_in), flops=2 * ROWS * D * 3 * D, name="qkv",
+        scratch=[TRANSPOSE_SCRATCH, pltpu.VMEM((D, 3 * D), bf16), pltpu.SemaphoreType.DMA((3,))],
     )
     qkv = to_peers(qkv_send, "seq")
     rows_all = lax.all_gather(rows_send, "seq", axis=0, tiled=True).reshape(SEQ, 2, 64, D + C_IN)
@@ -897,7 +908,7 @@
     gmi, qkv_rows, frames_normed = lax.optimization_barrier((gmi, qkv_rows, frames_normed))
     back_send, small_b = call(
         qkv_back_kernel, [shape((SEQ, 32, SW), bf16), Spill((8, D), f32)],
-        grad_qkv, Hbm(gmi), Hbm(conv_pre), Hbm(masked), Hbm(encoder_gain), Hbm(qkv_weight),
+        Smem(lengths), grad_qkv, Hbm(gmi), Hbm(conv_pre), Hbm(projected), Hbm(encoder_gain), Hbm(qkv_weight),
         scratch=[TRANSPOSE_SCRATCH], flops=2 * ROWS * D * 3 * D, name="qkv_back",
     )
     back_got = to_peers(back_send, "seq")

time: 239 us -> 238 us (level)
    unnamed x25 -> x23, local copies, waits for them, and re-layouts: 6.03 us -> 5.39 us
where the time goes in v1:
time: 238 us; the launch traced here: 234 us
  Pallas kernels  86.5 us (36%)
  starting transfers between devices  65.7 us (28%)
  blocking collectives  40.9 us (17%)
  waiting for transfers between devices  14.9 us (6%)
  between operations  14.8 us (6%)
  local copies, waits for them, and re-layouts  11.2 us (5%)
    pallas_call x17, Pallas kernels, call(): pl.pallas_call(wrapped, out_shape=[pltpu.HBM(o.struct.shape, o.struct.dty...  86.5 us
    all_to_all x3, blocking collectives, to_peers(): return lax.all_to_all(x, axis, 0, 0, tiled=True, axis_index_groups=groups)  40.9 us
    all_to_all x6, starting transfers between devices, to_peers(): return lax.all_to_all(x, axis, 0, 0, tiled=True, axis_index_groups=groups)  36.1 us
    ppermute x4, starting transfers between devices, local(): tap_got.append(lax.ppermute(piece, ('batch', 'seq'), moves))  20.4 us
    all_to_all x6, waiting for transfers between devices, to_peers(): return lax.all_to_all(x, axis, 0, 0, tiled=True, axis_index_groups=groups)  14.2 us
    ppermute x1, starting transfers between devices, local(): pair_got = lax.ppermute(pair_send, 'batch', swap)  6.35 us
    unnamed x23, local copies, waits for them, and re-layouts  5.39 us
  transfers between devices with their start and end apart: 16, of which 4 were waited for; matrix products, arithmetic and copies ran while one was open for 3% of the time, Pallas kernels for 32%

profile of v1, /device:TPU:1, one launch (start us, length us, event | category | flops | bytes accessed | tf_op | source)
XLA Modules:
  0.0 234.1 jit_solution(4706060318275314831)
XLA Ops:
  7.2 3.0 %project.1 = (f32[128,768]{1,0:T(8,128)}, bf16[16,16,384]{2,1,0:T(8,128)(2,1)}) custom-call(bf16[128,512]{1,0:T(8,128)(2,1)} %bitcast.16, bf16[512]{0:T(512)(128)(2,1)} %refs_2_.5, bf16[512]{0:T(512)(128)(2,1)} %refs_2_.4, bf16[512,768]{1,0:T(8,128)(2,1)} %refs_3_.7, bf16[768]{0:T(1024)(128)(2,1)} %refs_4_.3), custom_call_target="tpu_custom_call" | custom-call | flops 100663296 | bytes 1510912 | tf_op jit(solution)/shard_map/project/pallas_call | solution.py:228
  10.3 8.4 %all-to-all-start = ((bf16[16,16,384]{2,1,0:T(8,128)(2,1)}), bf16[16,16,384]{2,1,0:T(8,128)(2,1)S(1)}, u32[]{:S(2)}, u32[]{:S(2)}) async-start(bf16[16,16,384]{2,1,0:T(8,128)(2,1)} %get-tuple-element.82), calls=%async_computation | async-start | bytes 393216 | tf_op jit(solution)/shard_map/all_to_all | solution.py:816
  20.7 3.6 %reshape.81.refs_2_ = bf16[48,6144]{1,0:T(8,128)(2,1)} reshape(bf16[48,128,48]{2,1,0:T(8,128)(2,1)S(1)} %copy.50) | data formatting | bytes 1179648 | tf_op jit(solution)/shard_map/reshape | solution.py:839
  25.9 3.4 %conv.1 = (bf16[16,16,384]{2,1,0:T(8,128)(2,1)S(1)}, bf16[16,16,384]{2,1,0:T(8,128)(2,1)}) custom-call(s32[2]{0:T(128)S(1)} %copy-done.2, bf16[16,16,384]{2,1,0:T(8,128)(2,1)S(1)} %all-to-all-done.refs_1_, bf16[48,6144]{1,0:T(8,128)(2,1)} %reshape.81.refs_2_), custom_call_target="tpu_custom_call" | custom-call | flops 1283457024 | bytes 1179656 | tf_op jit(solution)/shard_map/conv/pallas_call | solution.py:228
  29.2 11.9 %all_to_all.49.refs_1_ = bf16[16,16,384]{2,1,0:T(8,128)(2,1)S(1)} all-to-all(bf16[16,16,384]{2,1,0:T(8,128)(2,1)S(1)} %get-tuple-element.83), channel_id=1, replica_groups=mesh['batch'=8,'seq'=16] {'seq'}, dimensions={0} | all-to-all | bytes 393216 | tf_op jit(solution)/shard_map/all_to_all | solution.py:816
  41.1 4.1 %qkv.1 = (f32[128,768]{1,0:T(8,128)}, f32[128,768]{1,0:T(8,128)}, bf16[16,192,128]{2,1,0:T(8,128)(2,1)}, bf16[128,1280]{1,0:T(8,128)(2,1)}) custom-call(s32[2]{0:T(128)S(1)} %copy-done.2, bf16[16,16,384]{2,1,0:T(8,128)(2,1)S(1)} %all_to_all.49.refs_1_, f32[128,768]{1,0:T(8,128)} %get-tuple-element.84.refs_2_.refs_4_, bf16[768]{0:T(1024)(128)(2,1)} %refs_3_.5, ...), custom_call_target="tpu_custom_call" | custom-call | flops 452984832 | bytes 6168072 | tf_op jit(solution)/shard_map/qkv/pallas_call | solution.py:228
  45.2 14.7 %all_to_all.50.refs_1_ = bf16[16,192,128]{2,1,0:T(8,128)(2,1)S(1)} all-to-all(bf16[16,192,128]{2,1,0:T(8,128)(2,1)} %get-tuple-element.85), channel_id=1, replica_groups=mesh['batch'=8,'seq'=16] {'seq'}, dimensions={0} | all-to-all | bytes 1572864 | tf_op jit(solution)/shard_map/all_to_all | solution.py:816
  59.9 5.9 %attend.1 = (bf16[1024,128]{1,0:T(8,128)(2,1)}, f32[1024,128]{1,0:T(8,128)}, f32[1024,128]{1,0:T(8,128)}, bf16[16,192,128]{2,1,0:T(8,128)(2,1)}) custom-call(s32[2]{0:T(128)S(1)} %copy-done.2, bf16[16,192,128]{2,1,0:T(8,128)(2,1)S(1)} %all_to_all.50.refs_1_), custom_call_target="tpu_custom_call" | custom-call | flops 1073741824 | bytes 2883592 | tf_op jit(solution)/shard_map/attend/pallas_call | solution.py:228
  65.8 4.1 %all-to-all-start.3 = ((bf16[16,64,128]{2,1,0:T(8,128)(2,1)}), bf16[16,64,128]{2,1,0:T(8,128)(2,1)S(1)}, u32[]{:S(2)}, u32[]{:S(2)}) async-start(bf16[16,64,128]{2,1,0:T(8,128)(2,1)} %bitcast.2), calls=%async_computation.3 | async-start | bytes 524288 | tf_op jit(solution)/shard_map/all_to_all | solution.py:816
  70.6 6.7 %all-to-all-done.3.refs_1_ = bf16[16,64,128]{2,1,0:T(8,128)(2,1)S(1)} async-done(((bf16[16,64,128]{2,1,0:T(8,128)(2,1)}), bf16[16,64,128]{2,1,0:T(8,128)(2,1)S(1)}, u32[]{:S(2)}, u32[]{:S(2)}) %all-to-all-start.3) | async-done | bytes 262176 | tf_op jit(solution)/shard_map/all_to_all | solution.py:816
  77.2 14.9 %middle.1 = (bf16[128,768]{1,0:T(8,128)(2,1)}, bf16[16,64,128]{2,1,0:T(8,128)(2,1)}, f32[128,768]{1,0:T(8,128)}, bf16[128,6912]{1,0:T(8,128)(2,1)S(1)}, bf16[128...) custom-call(s32[1]{0:T(128)S(6)} %copy.52.refs_0_, bf16[16,64,128]{2,1,0:T(8,128)(2,1)S(1)} %all-to-all-done.3.refs_1_, ...), custom_call_target="tpu_custom_call" | custom-call | flops 2717908992 | bytes 14744580 | tf_op jit(solution)/shard_map/middle/pallas_call | solution.py:228
  92.9 6.3 %collective-permute-start = (bf16[128,6912]{1,0:T(8,128)(2,1)S(1)}, bf16[128,6912]{1,0:T(8,128)(2,1)S(1)}, u32[]{:S(2)}, u32[]{:S(2)}) collective-permute-start(bf16[128,6912]{1,0:T(8,128)(2,1)S(1)} %get-tuple-element.91.refs_1_), channel_id=1, source_target_pairs={{0,16},{16,0},{32,48},{48,32},{64,80},{80,64},{96,112},{112,96},{1... | collective-permute-start | bytes 5308424 | tf_op jit(solution)/shard_map/ppermute | solution.py:884
  99.3 4.2 %all-to-all-start.4 = ((bf16[16,64,128]{2,1,0:T(8,128)(2,1)}), bf16[16,64,128]{2,1,0:T(8,128)(2,1)}, u32[]{:S(2)}, u32[]{:S(2)}) async-start(bf16[16,64,128]{2,1,0:T(8,128)(2,1)} %get-tuple-element.92), calls=%async_computation.4 | async-start | bytes 524288 | tf_op jit(solution)/shard_map/all_to_all | solution.py:816
  104.6 4.6 %dense_grads.1 = bf16[16,224,768]{2,1,0:T(8,128)(2,1)} custom-call(bf16[128,2304]{1,0:T(8,128)(2,1)S(1)} %copy-done.1, bf16[128,6912]{1,0:T(8,128)(2,1)S(1)} %get-tuple-element.91.refs_1_, bf16[128,6912]{1,0:T(8,128)(2,1)S(1)} %collective-permute-done.refs_2_), custom_call_target="tpu_custom_call" | custom-call | flops 1358954496 | bytes 9633792 | tf_op jit(solution)/shard_map/dense_grads/pallas_call | solution.py:228
  109.3 2.2 all-to-all-done.4
  111.5 10.8 %attend_back.1.refs_1_ = bf16[16,192,128]{2,1,0:T(8,128)(2,1)} custom-call(s32[2]{0:T(128)S(1)} %copy-done.2, bf16[16,192,128]{2,1,0:T(8,128)(2,1)} %get-tuple-element.89.refs_1_, bf16[1024,128]{1,0:T(8,128)(2,1)} %bitcast.5.refs_2_, f32[1024,128]{1,0:T(8,128)} %get-tuple-element.94.refs_3_, f32[1024,128]{1,0:T(8,128)} %get-tuple-element.95.refs_4_), custom_call_target="tpu_custom_call" | custom-call | flops 2684354560 | bytes 2883592 | tf_op jit(solution)/shard_map/attend_back/pallas_call | solution.py:228
  122.2 4.4 %all-to-all-start.5 = ((bf16[16,192,128]{2,1,0:T(8,128)(2,1)}), bf16[16,192,128]{2,1,0:T(8,128)(2,1)S(1)}, u32[]{:S(2)}, u32[]{:S(2)}) async-start(bf16[16,192,128]{2,1,0:T(8,128)(2,1)} %attend_back.1.refs_1_), calls=%async_computation.5 | async-start | bytes 1572864 | tf_op jit(solution)/shard_map/all_to_all | solution.py:816
  126.7 8.1 %frames.1 = (bf16[2048,512]{1,0:T(8,128)(2,1)}, bf16[2048,512]{1,0:T(8,128)(2,1)}, bf16[2048,512]{1,0:T(8,128)(2,1)}) custom-call(bf16[16,2,64,1280]{3,2,1,0:T(8,128)(2,1)} %bitcast.13, bf16[512]{0:T(512)(128)(2,1)} %refs_2_.5, bf16[512]{0:T(512)(128)(2,1)} %refs_2_.4), custom_call_target="tpu_custom_call" | custom-call | bytes 11536384 | tf_op jit(solution)/shard_map/frames/pallas_call | solution.py:228
  134.8 5.1 %head_grads.1.refs_7_ = bf16[1024,384]{1,0:T(8,128)(2,1)} custom-call(bf16[16,2,64,1280]{3,2,1,0:T(8,128)(2,1)} %bitcast.14, bf16[16,192,128]{2,1,0:T(8,128)(2,1)} %attend_back.1.refs_1_), custom_call_target="tpu_custom_call" | custom-call | flops 1207959552 | bytes 6815744 | tf_op jit(solution)/shard_map/head_grads/pallas_call | solution.py:228
  139.9 3.8 %all-to-all-done.5.refs_1_ = bf16[16,192,128]{2,1,0:T(8,128)(2,1)S(1)} async-done(((bf16[16,192,128]{2,1,0:T(8,128)(2,1)}), bf16[16,192,128]{2,1,0:T(8,128)(2,1)S(1)}, u32[]{:S(2)}, u32[]{:S(2)}) %all-to-all-start.5) | async-done | bytes 786464 | tf_op jit(solution)/shard_map/all_to_all | solution.py:816
  143.7 4.9 %qkv_back.1 = (bf16[16,32,384]{2,1,0:T(8,128)(2,1)S(1)}, f32[8,768]{1,0:T(8,128)}) custom-call(s32[2]{0:T(128)S(1)} %copy-done.2, bf16[16,192,128]{2,1,0:T(8,128)(2,1)S(1)} %all-to-all-done.5.refs_1_, f32[128,768]{1,0:T(8,128)} %get-tuple-element.99.refs_2_, f32[128,768]{1,0:T(8,128)} %get-tuple-element.100.refs_3_, ...), custom_call_target="tpu_custom_call" | custom-call | flops 452984832 | bytes 5924360 | tf_op jit(solution)/shard_map/qkv_back/pallas_call | solution.py:228
  148.7 14.4 %all_to_all.51.refs_1_.refs_0_ = bf16[16,32,384]{2,1,0:T(8,128)(2,1)S(1)} all-to-all(bf16[16,32,384]{2,1,0:T(8,128)(2,1)S(1)} %get-tuple-element.101), channel_id=1, replica_groups=mesh['batch'=8,'seq'=16] {'seq'}, dimensions={0} | all-to-all | bytes 786432 | tf_op jit(solution)/shard_map/all_to_all | solution.py:816
  163.0 2.7 %collective-permute-start.1 = (bf16[16,32,384]{2,1,0:T(8,128)(2,1)S(1)}, bf16[16,32,384]{2,1,0:T(8,128)(2,1)S(1)}, u32[]{:S(2)}, u32[]{:S(2)}) collective-permute-start(bf16[16,32,384]{2,1,0:T(8,128)(2,1)S(1)} %all_to_all.51.refs_1_.refs_0_), channel_id=1, source_target_pairs={{0,16},{16,0},{32,48},{48,32},{64,80},{80,64},{96,112},{112,96},{1... | collective-permute-start | bytes 1179656 | tf_op jit(solution)/shard_map/ppermute | solution.py:915
  165.8 5.1 %conv_back.1.refs_0_ = bf16[16,16,384]{2,1,0:T(8,128)(2,1)} custom-call(s32[2]{0:T(128)S(1)} %copy-done.2, bf16[16,32,384]{2,1,0:T(8,128)(2,1)} %copy-done.3, bf16[48,6144]{1,0:T(8,128)(2,1)} %reshape.81.refs_2_), custom_call_target="tpu_custom_call" | custom-call | flops 1283457024 | bytes 1179656 | tf_op jit(solution)/shard_map/conv_back/pallas_call | solution.py:228
  170.8 3.8 %all-to-all-start.7 = ((bf16[16,16,384]{2,1,0:T(8,128)(2,1)}), bf16[16,16,384]{2,1,0:T(8,128)(2,1)S(1)}, u32[]{:S(2)}, u32[]{:S(2)}) async-start(bf16[16,16,384]{2,1,0:T(8,128)(2,1)} %conv_back.1.refs_0_), calls=%async_computation.7 | async-start | bytes 393216 | tf_op jit(solution)/shard_map/all_to_all | solution.py:816
  174.7 6.1 %tail.1 = bf16[1024,384]{1,0:T(8,128)(2,1)} custom-call(bf16[16,16,384]{2,1,0:T(8,128)(2,1)} %conv_back.1.refs_0_, f32[16,768]{1,0:T(8,128)} %get-tuple-element.102.refs_1_, f32[8,768]{1,0:T(8,128)} %get-tuple-element.103.refs_2_, bf16[512,768]{1,0:T(8,128)(2,1)} %refs_3_.7, bf16[2048,512]{1,0:T(8,128)(2,1)} %get-tuple-element.104.refs_4_, ...), custom_call_target="tpu_custom_call" | custom-call | flops 805306368 | bytes 8921088 | tf_op jit(solution)/shard_map/tail/pallas_call | solution.py:228
  182.3 4.5 %conv_grads.1 = (bf16[48,768]{1,0:T(8,128)(2,1)}, bf16[48,768]{1,0:T(8,128)(2,1)}, bf16[48,768]{1,0:T(8,128)(2,1)}, bf16[48,768]{1,0:T(8,128)(2,1)}) custom-call(bf16[16,32,384]{2,1,0:T(8,128)(2,1)} %copy-done.3, bf16[16,32,384]{2,1,0:T(8,128)(2,1)} %copy-done.8, bf16[16,16,384]{2,1,0:T(8,128)(2,1)} %get-tuple-element.108.refs_2_, ...), custom_call_target="tpu_custom_call" | custom-call | flops 1283457024 | bytes 1474560 | tf_op jit(solution)/shard_map/conv_grads/pallas_call | solution.py:228
  186.7 11.1 %all-to-all-start.8 = ((bf16[128,8,384]{2,1,0:T(8,128)(2,1)}), bf16[128,8,384]{2,1,0:T(8,128)(2,1)S(1)}, u32[]{:S(2)}, u32[]{:S(2)}) async-start(bf16[128,8,384]{2,1,0:T(8,128)(2,1)} %bitcast.8), calls=%async_computation.8 | async-start | bytes 1572864 | tf_op jit(solution)/shard_map/all_to_all | solution.py:816
  198.6 3.7 %collective-permute-start.3 = (bf16[48,768]{1,0:T(8,128)(2,1)}, bf16[48,768]{1,0:T(8,128)(2,1)S(1)}, u32[]{:S(2)}, u32[]{:S(2)}) collective-permute-start(bf16[48,768]{1,0:T(8,128)(2,1)} %get-tuple-element.120), channel_id=1, source_target_pairs={{0,0},{1,8},{2,16},{3,24},{4,32},{5,40},{6,48},{7,56},{8,64},{9,72... | collective-permute-start | bytes 221192 | tf_op jit(solution)/shard_map/ppermute | solution.py:946
  202.3 5.7 %collective-permute-start.4 = (bf16[48,768]{1,0:T(8,128)(2,1)}, bf16[48,768]{1,0:T(8,128)(2,1)S(1)}, u32[]{:S(2)}, u32[]{:S(2)}) collective-permute-start(bf16[48,768]{1,0:T(8,128)(2,1)} %get-tuple-element.121), channel_id=1, source_target_pairs={{0,2},{1,10},{2,18},{3,26},{4,34},{5,42},{6,50},{7,58},{8,66},{9,7... | collective-permute-start | bytes 221192 | tf_op jit(solution)/shard_map/ppermute | solution.py:946
  210.1 9.0 %collective-permute-start.6 = (bf16[48,768]{1,0:T(8,128)(2,1)}, bf16[48,768]{1,0:T(8,128)(2,1)S(1)}, u32[]{:S(2)}, u32[]{:S(2)}) collective-permute-start(bf16[48,768]{1,0:T(8,128)(2,1)} %get-tuple-element.123), channel_id=1, source_target_pairs={{0,6},{1,14},{2,22},{3,30},{4,38},{5,46},{6,54},{7,62},{8,70},{9,7... | collective-permute-start | bytes 221192 | tf_op jit(solution)/shard_map/ppermute | solution.py:946
  219.1 2.6 %feats_back.1 = f32[128,512]{1,0:T(8,128)} custom-call(bf16[16,16,384]{2,1,0:T(8,128)(2,1)S(1)} %all-to-all-done.7.refs_0_, bf16[128,512]{1,0:T(8,128)(2,1)} %bitcast.18, bf16[512]{0:T(512)(128)(2,1)} %refs_2_.5, bf16[512,768]{1,0:T(8,128)(2,1)} %refs_3_.7), custom_call_target="tpu_custom_call" | custom-call | flops 100663296 | bytes 1377280 | tf_op jit(solution)/shard_map/feats_back/pallas_call | solution.py:228
  (50 shorter events, 15.5 us)
Async XLA Ops:
  7.2 18.7 %copy-start.2 = (s32[2]{0:T(128)S(1)}, s32[2]{0:T(128)}, u32[]{:S(2)}) copy-start(s32[2]{0:T(128)} %refs_0_.12) | copy-start | bytes 28
  10.3 15.6 %all-to-all-start = ((bf16[16,16,384]{2,1,0:T(8,128)(2,1)}), bf16[16,16,384]{2,1,0:T(8,128)(2,1)S(1)}, u32[]{:S(2)}, u32[]{:S(2)}) async-start(bf16[16,16,384]{2,1,0:T(8,128)(2,1)} %get-tuple-element.82), calls=%async_computation | async-start | bytes 393216 | tf_op jit(solution)/shard_map/all_to_all | solution.py:816
  18.7 108.0 %all-gather.2.cloned.1.call-start = ((), (), s32[]{:S(2)}) async-start(), calls=%async_computation.11 | async-start | bytes 5570560 | tf_op jit(solution)/shard_map/all_gather | solution.py:860
  65.8 11.4 %all-to-all-start.3 = ((bf16[16,64,128]{2,1,0:T(8,128)(2,1)}), bf16[16,64,128]{2,1,0:T(8,128)(2,1)S(1)}, u32[]{:S(2)}, u32[]{:S(2)}) async-start(bf16[16,64,128]{2,1,0:T(8,128)(2,1)} %bitcast.2), calls=%async_computation.3 | async-start | bytes 524288 | tf_op jit(solution)/shard_map/all_to_all | solution.py:816
  92.1 0.8 copy-start
  92.9 10.6 %collective-permute-start = (bf16[128,6912]{1,0:T(8,128)(2,1)S(1)}, bf16[128,6912]{1,0:T(8,128)(2,1)S(1)}, u32[]{:S(2)}, u32[]{:S(2)}) collective-permute-start(bf16[128,6912]{1,0:T(8,128)(2,1)S(1)} %get-tuple-element.91.refs_1_), channel_id=1, source_target_pairs={{0,16},{16,0},{32,48},{48,32},{64,80},{80,64},{96,112},{112,96},{1... | collective-permute-start | bytes 5308424 | tf_op jit(solution)/shard_map/ppermute | solution.py:884
  99.3 12.2 %all-to-all-start.4 = ((bf16[16,64,128]{2,1,0:T(8,128)(2,1)}), bf16[16,64,128]{2,1,0:T(8,128)(2,1)}, u32[]{:S(2)}, u32[]{:S(2)}) async-start(bf16[16,64,128]{2,1,0:T(8,128)(2,1)} %get-tuple-element.92), calls=%async_computation.4 | async-start | bytes 524288 | tf_op jit(solution)/shard_map/all_to_all | solution.py:816
  103.5 94.5 %reduce-scatter.3.cloned.1.call-start = ((), (), s32[]{:S(2)}) async-start(), calls=%async_computation.12 | async-start | bytes 5849088 | tf_op jit(solution)/shard_map/reduce_scatter | solution.py:891
  103.5 1.1 copy-start.1
  122.2 21.5 %all-to-all-start.5 = ((bf16[16,192,128]{2,1,0:T(8,128)(2,1)}), bf16[16,192,128]{2,1,0:T(8,128)(2,1)S(1)}, u32[]{:S(2)}, u32[]{:S(2)}) async-start(bf16[16,192,128]{2,1,0:T(8,128)(2,1)} %attend_back.1.refs_1_), calls=%async_computation.5 | async-start | bytes 1572864 | tf_op jit(solution)/shard_map/all_to_all | solution.py:816
  139.9 25.8 %copy-start.9 = (bf16[16,16,384]{2,1,0:T(8,128)(2,1)S(1)}, bf16[16,16,384]{2,1,0:T(8,128)(2,1)}, u32[]{:S(2)}) copy-start(bf16[16,16,384]{2,1,0:T(8,128)(2,1)} %get-tuple-element.108.refs_2_) | copy-start | bytes 589828
  163.0 2.7 %copy-start.3 = (bf16[16,32,384]{2,1,0:T(8,128)(2,1)}, bf16[16,32,384]{2,1,0:T(8,128)(2,1)S(1)}, u32[]{:S(2)}) copy-start(bf16[16,32,384]{2,1,0:T(8,128)(2,1)S(1)} %all_to_all.51.refs_1_.refs_0_) | copy-start | bytes 1179652
  163.0 17.8 %collective-permute-start.1 = (bf16[16,32,384]{2,1,0:T(8,128)(2,1)S(1)}, bf16[16,32,384]{2,1,0:T(8,128)(2,1)S(1)}, u32[]{:S(2)}, u32[]{:S(2)}) collective-permute-start(bf16[16,32,384]{2,1,0:T(8,128)(2,1)S(1)} %all_to_all.51.refs_1_.refs_0_), channel_id=1, source_target_pairs={{0,16},{16,0},{32,48},{48,32},{64,80},{80,64},{96,112},{112,96},{1... | collective-permute-start | bytes 1179656 | tf_op jit(solution)/shard_map/ppermute | solution.py:915
  165.7 15.1 %collective-permute-start.2 = (bf16[16,16,384]{2,1,0:T(8,128)(2,1)S(1)}, bf16[16,16,384]{2,1,0:T(8,128)(2,1)S(1)}, u32[]{:S(2)}, u32[]{:S(2)}) collective-permute-start(bf16[16,16,384]{2,1,0:T(8,128)(2,1)S(1)} %copy-done.9), channel_id=1, source_target_pairs={{0,16},{16,0},{32,48},{48,32},{64,80},{80,64},{96,112},{112,96},{1... | collective-permute-start | bytes 589832 | tf_op jit(solution)/shard_map/ppermute | solution.py:916
  170.8 15.9 %all-to-all-start.7 = ((bf16[16,16,384]{2,1,0:T(8,128)(2,1)}), bf16[16,16,384]{2,1,0:T(8,128)(2,1)S(1)}, u32[]{:S(2)}, u32[]{:S(2)}) async-start(bf16[16,16,384]{2,1,0:T(8,128)(2,1)} %conv_back.1.refs_0_), calls=%async_computation.7 | async-start | bytes 393216 | tf_op jit(solution)/shard_map/all_to_all | solution.py:816
  180.8 0.7 copy-start.10
  181.5 0.8 copy-start.8
  186.7 38.3 %all-to-all-start.8 = ((bf16[128,8,384]{2,1,0:T(8,128)(2,1)}), bf16[128,8,384]{2,1,0:T(8,128)(2,1)S(1)}, u32[]{:S(2)}, u32[]{:S(2)}) async-start(bf16[128,8,384]{2,1,0:T(8,128)(2,1)} %bitcast.8), calls=%async_computation.8 | async-start | bytes 1572864 | tf_op jit(solution)/shard_map/all_to_all | solution.py:816
  197.9 28.1 %reduce-scatter.5.cloned.1.call-start = ((), (), s32[]{:S(2)}) async-start(), calls=%async_computation.13 | async-start | bytes 430080 | tf_op jit(solution)/shard_map/reduce_scatter | solution.py:950
  198.6 23.1 %collective-permute-start.3 = (bf16[48,768]{1,0:T(8,128)(2,1)}, bf16[48,768]{1,0:T(8,128)(2,1)S(1)}, u32[]{:S(2)}, u32[]{:S(2)}) collective-permute-start(bf16[48,768]{1,0:T(8,128)(2,1)} %get-tuple-element.120), channel_id=1, source_target_pairs={{0,0},{1,8},{2,16},{3,24},{4,32},{5,40},{6,48},{7,56},{8,64},{9,72... | collective-permute-start | bytes 221192 | tf_op jit(solution)/shard_map/ppermute | solution.py:946
  202.3 19.4 %collective-permute-start.4 = (bf16[48,768]{1,0:T(8,128)(2,1)}, bf16[48,768]{1,0:T(8,128)(2,1)S(1)}, u32[]{:S(2)}, u32[]{:S(2)}) collective-permute-start(bf16[48,768]{1,0:T(8,128)(2,1)} %get-tuple-element.121), channel_id=1, source_target_pairs={{0,2},{1,10},{2,18},{3,26},{4,34},{5,42},{6,50},{7,58},{8,66},{9,7... | collective-permute-start | bytes 221192 | tf_op jit(solution)/shard_map/ppermute | solution.py:946
  208.0 13.7 %collective-permute-start.5 = (bf16[48,768]{1,0:T(8,128)(2,1)}, bf16[48,768]{1,0:T(8,128)(2,1)S(1)}, u32[]{:S(2)}, u32[]{:S(2)}) collective-permute-start(bf16[48,768]{1,0:T(8,128)(2,1)} %get-tuple-element.122), channel_id=1, source_target_pairs={{0,4},{1,12},{2,20},{3,28},{4,36},{5,44},{6,52},{7,60},{8,68},{9,7... | collective-permute-start | bytes 221192 | tf_op jit(solution)/shard_map/ppermute | solution.py:946
  210.1 11.7 %collective-permute-start.6 = (bf16[48,768]{1,0:T(8,128)(2,1)}, bf16[48,768]{1,0:T(8,128)(2,1)S(1)}, u32[]{:S(2)}, u32[]{:S(2)}) collective-permute-start(bf16[48,768]{1,0:T(8,128)(2,1)} %get-tuple-element.123), channel_id=1, source_target_pairs={{0,6},{1,14},{2,22},{3,30},{4,38},{5,46},{6,54},{7,62},{8,70},{9,7... | collective-permute-start | bytes 221192 | tf_op jit(solution)/shard_map/ppermute | solution.py:946
  221.7 0.6 copy-start.4
  221.7 0.6 copy-start.5
  221.8 0.6 copy-start.6
  222.4 0.6 copy-start.7
Sparse Core Ops, SparseCore 0:
  45.4 58.8 all-gather.1
  111.6 86.1 reduce-scatter.2
  201.1 24.3 reduce-scatter.4
